TPU v7x, 256 devices: a whole 4x4x8 slice. The times are simulated.
256 devices in a mesh: ctx: 16 (over y, z_hi), head: 4 (over z_lo, core), dp: 4 (over x).
Axes of the slice: x: 4, y: 4, z: 8 (z_hi: 4, z_lo: 2; z = z_hi * 2 + z_lo), core: 2. Of those that a mesh axis runs over, the one named last changes fastest.
Arguments:
- query_rows: bfloat16 [32768, 4096], P(('dp', 'ctx', 'head')), parts along dimension 0, may hold values from -6 to 6
- key_rows: bfloat16 [32768, 512], P(('dp', 'ctx', 'head')), parts along dimension 0, may hold values from -6 to 6
- value_rows: bfloat16 [32768, 512], P(('dp', 'ctx', 'head')), parts along dimension 0, may hold values from -6 to 6
- fwd_output: bfloat16 [32768, 4096], P(('dp', 'ctx', 'head')), parts along dimension 0, may hold values from -6 to 6
- grad_output: bfloat16 [32768, 4096], P(('dp', 'ctx', 'head')), parts along dimension 0, may hold values from -6 to 6
- log_normalizer: float32 [32768, 32], P(('dp', 'ctx', 'head')), parts along dimension 0, may hold values from -1 to 12
- doc_lengths: int32 [24], P('dp'), parts along dimension 0, may hold values from 256 to 2048, as said below
Outputs:
- grad_query: bfloat16 [32768, 4096], P(('dp', 'ctx', 'head')), parts along dimension 0
- grad_key: bfloat16 [32768, 512], P(('dp', 'ctx', 'head')), parts along dimension 0
- grad_value: bfloat16 [32768, 512], P(('dp', 'ctx', 'head')), parts along dimension 0
There are 4 independent parts, one for each index of `dp`. A program takes and returns all parts, laid end to end along the dimension named above; each array names one. Nothing has to cross between parts.
Inputs may be any that keep to these rules, and one draw needn't show every extreme that they name: `doc_lengths`: the 6 lengths sum to 8192; the largest is exactly 2048.
All inputs are finite; a program needn't handle non-finite values.
Results may differ from a plain program's by a relative error of at most 0.0053.
Values may be sent and summed in bfloat16 or wider, within the bound.
A program may use at most 64 MiB of HBM per device.

v0:
```python
import jax
import jax.numpy as jnp
from jax import lax
from jax.sharding import PartitionSpec as P

HD = 128


def from_behind(array, axis, by):
    peers = lax.axis_size(axis)
    pairs = [(i, i + by) for i in range(peers) if 0 <= i + by < peers]
    return lax.ppermute(array, axis, pairs)


def from_behind_2(block, axis, distance):
    devices = range(lax.axis_size(axis))
    route = [((i - distance) % len(devices), i) for i in devices]
    return lax.ppermute(block, axis, route)


def doc_index(positions, doc_ends):
    return jnp.sum((positions[:, None] >= doc_ends[None, :]).astype(jnp.int32), axis=1)


def block_terms(query_blk, grad_blk, norm_blk, delta_blk, key_blk, value_blk, allowed):
    row_count = query_blk.shape[0]
    col_count = key_blk.shape[0]
    kv_local = key_blk.shape[1] // HD
    group = query_blk.shape[1] // key_blk.shape[1]
    score_scale = HD ** (-0.5)
    query_four = query_blk.reshape(row_count, kv_local, group, HD)
    grad_four = grad_blk.reshape(row_count, kv_local, group, HD)
    key_three = key_blk.reshape(col_count, kv_local, HD)
    value_three = value_blk.reshape(col_count, kv_local, HD)
    norm_four = norm_blk.reshape(row_count, kv_local, group).transpose(1, 2, 0)[..., None]
    delta_four = delta_blk.reshape(row_count, kv_local, group).transpose(1, 2, 0)[..., None]
    scores = (
        jnp.einsum("ikgd,jkd->kgij", query_four, key_three, preferred_element_type=jnp.float32)
        * score_scale
    )
    probs = jnp.where(allowed[None, None], jnp.exp(scores - norm_four), 0.0)
    probs_half = probs.astype(jnp.bfloat16)
    value_term = jnp.einsum(
        "kgij,ikgd->jkd", probs_half, grad_four, preferred_element_type=jnp.float32
    )
    grad_probs = jnp.einsum(
        "ikgd,jkd->kgij", grad_four, value_three, preferred_element_type=jnp.float32
    )
    grad_scores = (probs * (grad_probs - delta_four)).astype(jnp.bfloat16)
    query_term = (
        jnp.einsum("kgij,jkd->ikgd", grad_scores, key_three, preferred_element_type=jnp.float32)
        * score_scale
    )
    key_term = (
        jnp.einsum("kgij,ikgd->jkd", grad_scores, query_four, preferred_element_type=jnp.float32)
        * score_scale
    )
    return (
        query_term.reshape(row_count, -1),
        key_term.reshape(col_count, -1),
        value_term.reshape(col_count, -1),
    )


def body(query_rows, key_rows, value_rows, fwd_output, grad_output, log_normalizer, doc_lengths):
    entry_rows = query_rows.shape[0]
    delta_rows = jnp.sum(
        (fwd_output.astype(jnp.float32) * grad_output.astype(jnp.float32)).reshape(
            entry_rows, -1, HD
        ),
        axis=-1,
    )
    query_blk, grad_blk = (
        lax.all_to_all(query_rows, "head", split_axis=1, concat_axis=0, tiled=True),
        lax.all_to_all(grad_output, "head", split_axis=1, concat_axis=0, tiled=True),
    )
    key_blk, value_blk = (
        lax.all_to_all(key_rows, "head", split_axis=1, concat_axis=0, tiled=True),
        lax.all_to_all(value_rows, "head", split_axis=1, concat_axis=0, tiled=True),
    )
    norm_blk, delta_blk = (
        lax.all_to_all(log_normalizer, "head", split_axis=1, concat_axis=0, tiled=True),
        lax.all_to_all(delta_rows, "head", split_axis=1, concat_axis=0, tiled=True),
    )
    block_rows = query_blk.shape[0]
    cycle_size = lax.axis_size("ctx")
    cycle_place = lax.axis_index("ctx")
    doc_ends = jnp.cumsum(doc_lengths)
    offsets = jnp.arange(block_rows, dtype=jnp.int32)
    query_pos = cycle_place * block_rows + offsets
    query_doc = doc_index(query_pos, doc_ends)

    def visit(anchor, key_cur, value_cur):
        key_pos = anchor * block_rows + offsets
        key_doc = doc_index(key_pos, doc_ends)
        allowed = (key_pos[None, :] <= query_pos[:, None]) & (
            key_doc[None, :] == query_doc[:, None]
        )

        def compute_terms():
            return block_terms(
                query_blk, grad_blk, norm_blk, delta_blk, key_cur, value_cur, allowed
            )

        def empty_terms():
            return (
                jnp.zeros(query_blk.shape, jnp.float32),
                jnp.zeros(key_cur.shape, jnp.float32),
                jnp.zeros(value_cur.shape, jnp.float32),
            )

        return lax.cond(jnp.any(allowed), compute_terms, empty_terms)

    query_zero = jnp.zeros(query_blk.shape, jnp.float32)

    def travel_turn(turn, carry):
        key_cur, value_cur, key_acc, value_acc, query_acc = carry
        anchor = (cycle_place - turn) % cycle_size
        query_term, key_term, value_term = visit(anchor, key_cur, value_cur)
        key_cur, value_cur = from_behind((key_cur, value_cur), "ctx", 1)
        key_acc, value_acc = from_behind_2((key_acc + key_term, value_acc + value_term), "ctx", 1)
        return (key_cur, value_cur, key_acc, value_acc, query_acc + query_term)

    start_carry = (
        key_blk,
        value_blk,
        jnp.zeros(key_blk.shape, jnp.float32),
        jnp.zeros(value_blk.shape, jnp.float32),
        query_zero,
    )
    final_carry = lax.fori_loop(0, cycle_size, travel_turn, start_carry)
    key_sum, value_sum, query_acc = (final_carry[2], final_carry[3], final_carry[4])
    grad_query, grad_key, grad_value = (
        lax.all_to_all(
            query_acc.astype(jnp.bfloat16), "head", split_axis=0, concat_axis=1, tiled=True
        ),
        lax.all_to_all(
            key_sum.astype(jnp.bfloat16), "head", split_axis=0, concat_axis=1, tiled=True
        ),
        lax.all_to_all(
            value_sum.astype(jnp.bfloat16), "head", split_axis=0, concat_axis=1, tiled=True
        ),
    )
    return (grad_query, grad_key, grad_value)


def solution(mesh):
    placed = (
        P(("dp", "ctx", "head"), None),
        P(("dp", "ctx", "head"), None),
        P(("dp", "ctx", "head"), None),
        P(("dp", "ctx", "head"), None),
        P(("dp", "ctx", "head"), None),
        P(("dp", "ctx", "head"), None),
        P("dp"),
    )
    return jax.shard_map(
        body,
        mesh=mesh,
        in_specs=placed,
        out_specs=(
            P(("dp", "ctx", "head"), None),
            P(("dp", "ctx", "head"), None),
            P(("dp", "ctx", "head"), None),
        ),
        check_vma=False,
    )
```

profile of v0, /device:TPU:1, one launch (start us, length us, event | category | flops | bytes accessed | tf_op | source)
XLA Modules:
  0.0 806.5 jit_solution(325672444785577632)
XLA Ops:
  0.6 7.2 all-to-all-start.3
  11.3 4.3 all-to-all-start.5
  18.9 4.0 all-to-all-start
  26.5 4.9 all-to-all-start.1
  35.1 4.5 all-to-all-start.2
  42.0 11.3 %all-to-all-done.2 = bf16[128,4,1024]{2,0,1:T(8,128)(2,1)S(1)} async-done(((bf16[128,4,1024]{2,0,1:T(8,128)(2,1)}), bf16[128,4,1024]{2,0,1:T(8,128)(2,1)S(1)}, u32[]{:S(2)}, u32[]{:S(2)}) %all-to-all-start.2) | async-done | bytes 1048608 | tf_op jit(solution)/shard_map/all_to_all | solution.py:74
  53.2 5.1 all-to-all-start.4
  59.5 12.5 %all-to-all-done.4 = bf16[128,4,1024]{2,0,1:T(8,128)(2,1)} async-done(((bf16[128,4,1024]{2,0,1:T(8,128)(2,1)}), bf16[128,4,1024]{2,0,1:T(8,128)(2,1)}, u32[]{:S(2)}, u32[]{:S(2)}) %all-to-all-start.4) | async-done | bytes 1048608 | tf_op jit(solution)/shard_map/all_to_all | solution.py:75
  73.5 696.0 %while.24 = (s32[]{:T(128)}, bf16[512,128]{0,1:T(8,128)(2,1)}, bf16[512,128]{1,0:T(8,128)(2,1)}, f32[512,128]{1,0:T(8,128)}, f32[512,128]{1,0:T(8,128)}, /*index...) while((s32[]{:T(128)}, bf16[512,128]{0,1:T(8,128)(2,1)}, ...), condition=%wide.region_8.9_spmd.clone, body=%wide.region_3.8_spmd.clone.sunk | while | flops 2708153856 | bytes 58393196 | solution.py:131
  80.4 6.1 collective-permute-start.1
  88.9 12.3 %conditional.3 = (f32[512,1024]{0,1:T(8,128)S(1)}, f32[512,128]{1,0:T(8,128)S(1)}, f32[512,128]{1,0:T(8,128)S(1)}) conditional(s32[]{:T(128)} %convert_element_type.68, () %tuple.63, (pred[512,512]{0,1:T(8,128)(4,1)}, bf16[512,1024]{1,0:T(8,128)(2,1)S(1)}, bf16[512,128]{0,1:T(8,128)(2,1)}, f32[512,8]{0,1:T(8,128)}, bf16[512,1024]{1,0:T(8,128)(2,1)}, ...), branch_computations={%region_6.6_spmd, %region_7.7_spmd} | conditional | flops 2705915904 | bytes 46579764 | solution.py:112
  94.1 4.2 fusion.10
  106.4 12.4 %collective-permute-done.3 = f32[512,128]{1,0:T(8,128)} collective-permute-done((f32[512,128]{1,0:T(8,128)}, f32[512,128]{1,0:T(8,128)}, u32[]{:S(2)}, u32[]{:S(2)}) %collective-permute-start.3) | collective-permute-done | bytes 262176 | tf_op jit(solution)/shard_map/while/body/eval_jaxpr/ppermute | solution.py:18
  118.7 11.6 %collective-permute-done.2 = f32[512,128]{1,0:T(8,128)} collective-permute-done((f32[512,128]{1,0:T(8,128)S(1)}, f32[512,128]{1,0:T(8,128)}, u32[]{:S(2)}, u32[]{:S(2)}) %collective-permute-start.2) | collective-permute-done | bytes 262176 | tf_op jit(solution)/shard_map/while/body/eval_jaxpr/ppermute | solution.py:18
  141.7 7.5 collective-permute-start.3
  150.3 5.5 collective-permute-start.2
  159.2 9.0 %collective-permute-done.2 = f32[512,128]{1,0:T(8,128)} collective-permute-done((f32[512,128]{1,0:T(8,128)S(1)}, f32[512,128]{1,0:T(8,128)}, u32[]{:S(2)}, u32[]{:S(2)}) %collective-permute-start.2) | collective-permute-done | bytes 262176 | tf_op jit(solution)/shard_map/while/body/eval_jaxpr/ppermute | solution.py:18
  173.3 5.0 collective-permute-start.1
  183.7 11.4 %collective-permute-start.2 = (f32[512,128]{1,0:T(8,128)S(1)}, f32[512,128]{1,0:T(8,128)}, u32[]{:S(2)}, u32[]{:S(2)}) collective-permute-start(f32[512,128]{1,0:T(8,128)S(1)} %add.139), channel_id=1, source_target_pairs={{240,0},{0,16},{16,32},{32,48},{48,64},{64,80},{80,96},{96,112},{1... | collective-permute-start | bytes 786440 | tf_op jit(solution)/shard_map/while/body/eval_jaxpr/ppermute | solution.py:18
  198.6 4.3 collective-permute-done.2
  204.5 5.8 collective-permute-start
  221.6 5.0 collective-permute-start.2
  230.1 10.9 %collective-permute-done.3 = f32[512,128]{1,0:T(8,128)} collective-permute-done((f32[512,128]{1,0:T(8,128)}, f32[512,128]{1,0:T(8,128)}, u32[]{:S(2)}, u32[]{:S(2)}) %collective-permute-start.3) | collective-permute-done | bytes 262176 | tf_op jit(solution)/shard_map/while/body/eval_jaxpr/ppermute | solution.py:18
  256.6 8.1 %collective-permute-start.2 = (f32[512,128]{1,0:T(8,128)S(1)}, f32[512,128]{1,0:T(8,128)}, u32[]{:S(2)}, u32[]{:S(2)}) collective-permute-start(f32[512,128]{1,0:T(8,128)S(1)} %add.139), channel_id=1, source_target_pairs={{240,0},{0,16},{16,32},{32,48},{48,64},{64,80},{80,96},{96,112},{1... | collective-permute-start | bytes 786440 | tf_op jit(solution)/shard_map/while/body/eval_jaxpr/ppermute | solution.py:18
  268.1 24.4 %collective-permute-done.3 = f32[512,128]{1,0:T(8,128)} collective-permute-done((f32[512,128]{1,0:T(8,128)}, f32[512,128]{1,0:T(8,128)}, u32[]{:S(2)}, u32[]{:S(2)}) %collective-permute-start.3) | collective-permute-done | bytes 262176 | tf_op jit(solution)/shard_map/while/body/eval_jaxpr/ppermute | solution.py:18
  292.5 6.3 collective-permute-done.2
  314.7 10.5 %collective-permute-done.3 = f32[512,128]{1,0:T(8,128)} collective-permute-done((f32[512,128]{1,0:T(8,128)}, f32[512,128]{1,0:T(8,128)}, u32[]{:S(2)}, u32[]{:S(2)}) %collective-permute-start.3) | collective-permute-done | bytes 262176 | tf_op jit(solution)/shard_map/while/body/eval_jaxpr/ppermute | solution.py:18
  330.6 5.5 collective-permute-start
  337.7 5.8 collective-permute-start.1
  347.8 6.5 collective-permute-start.3
  355.3 5.3 collective-permute-start.2
  364.1 4.9 collective-permute-done.2
  370.6 31.5 %collective-permute-start = (bf16[512,128]{0,1:T(8,128)(2,1)}, bf16[512,128]{0,1:T(8,128)(2,1)}, u32[]{:S(2)}, u32[]{:S(2)}) collective-permute-start(bf16[512,128]{0,1:T(8,128)(2,1)} %copy.118), channel_id=1, source_target_pairs={{0,16},{16,32},{32,48},{48,64},{64,80},{80,96},{96,112},{112,128},... | collective-permute-start | bytes 393224 | tf_op jit(solution)/shard_map/while/body/eval_jaxpr/ppermute | solution.py:12
  403.7 11.6 %collective-permute-start.1 = (bf16[512,128]{1,0:T(8,128)(2,1)}, bf16[512,128]{1,0:T(8,128)(2,1)}, u32[]{:S(2)}, u32[]{:S(2)}) collective-permute-start(bf16[512,128]{1,0:T(8,128)(2,1)} %copy.119), channel_id=1, source_target_pairs={{0,16},{16,32},{32,48},{48,64},{64,80},{80,96},{96,112},{112,128},... | collective-permute-start | bytes 393224 | tf_op jit(solution)/shard_map/while/body/eval_jaxpr/ppermute | solution.py:12
  428.3 4.5 collective-permute-done.3
  432.8 11.1 %collective-permute-done.2 = f32[512,128]{1,0:T(8,128)} collective-permute-done((f32[512,128]{1,0:T(8,128)S(1)}, f32[512,128]{1,0:T(8,128)}, u32[]{:S(2)}, u32[]{:S(2)}) %collective-permute-start.2) | collective-permute-done | bytes 262176 | tf_op jit(solution)/shard_map/while/body/eval_jaxpr/ppermute | solution.py:18
  448.9 5.1 collective-permute-start.1
  471.2 12.4 %collective-permute-done.2 = f32[512,128]{1,0:T(8,128)} collective-permute-done((f32[512,128]{1,0:T(8,128)S(1)}, f32[512,128]{1,0:T(8,128)}, u32[]{:S(2)}, u32[]{:S(2)}) %collective-permute-start.2) | collective-permute-done | bytes 262176 | tf_op jit(solution)/shard_map/while/body/eval_jaxpr/ppermute | solution.py:18
  485.2 5.8 collective-permute-start
  492.5 4.4 collective-permute-start.1
  511.1 6.3 collective-permute-done.2
  519.0 5.9 collective-permute-start
  538.6 6.9 collective-permute-done.3
  553.4 4.7 collective-permute-start.1
  563.5 5.4 collective-permute-start.2
  573.6 7.4 collective-permute-done.2
  594.0 5.0 collective-permute-start.3
  600.0 10.2 %collective-permute-start.2 = (f32[512,128]{1,0:T(8,128)S(1)}, f32[512,128]{1,0:T(8,128)}, u32[]{:S(2)}, u32[]{:S(2)}) collective-permute-start(f32[512,128]{1,0:T(8,128)S(1)} %add.139), channel_id=1, source_target_pairs={{240,0},{0,16},{16,32},{32,48},{48,64},{64,80},{80,96},{96,112},{1... | collective-permute-start | bytes 786440 | tf_op jit(solution)/shard_map/while/body/eval_jaxpr/ppermute | solution.py:18
  616.5 5.8 collective-permute-start
  623.9 13.2 %collective-permute-start.1 = (bf16[512,128]{1,0:T(8,128)(2,1)}, bf16[512,128]{1,0:T(8,128)(2,1)}, u32[]{:S(2)}, u32[]{:S(2)}) collective-permute-start(bf16[512,128]{1,0:T(8,128)(2,1)} %copy.119), channel_id=1, source_target_pairs={{0,16},{16,32},{32,48},{48,64},{64,80},{80,96},{96,112},{112,128},... | collective-permute-start | bytes 393224 | tf_op jit(solution)/shard_map/while/body/eval_jaxpr/ppermute | solution.py:12
  645.1 12.2 %collective-permute-start.2 = (f32[512,128]{1,0:T(8,128)S(1)}, f32[512,128]{1,0:T(8,128)}, u32[]{:S(2)}, u32[]{:S(2)}) collective-permute-start(f32[512,128]{1,0:T(8,128)S(1)} %add.139), channel_id=1, source_target_pairs={{240,0},{0,16},{16,32},{32,48},{48,64},{64,80},{80,96},{96,112},{1... | collective-permute-start | bytes 786440 | tf_op jit(solution)/shard_map/while/body/eval_jaxpr/ppermute | solution.py:18
  660.7 5.0 collective-permute-done.2
  667.3 15.4 %collective-permute-start = (bf16[512,128]{0,1:T(8,128)(2,1)}, bf16[512,128]{0,1:T(8,128)(2,1)}, u32[]{:S(2)}, u32[]{:S(2)}) collective-permute-start(bf16[512,128]{0,1:T(8,128)(2,1)} %copy.118), channel_id=1, source_target_pairs={{0,16},{16,32},{32,48},{48,64},{64,80},{80,96},{96,112},{112,128},... | collective-permute-start | bytes 393224 | tf_op jit(solution)/shard_map/while/body/eval_jaxpr/ppermute | solution.py:12
  684.2 6.3 collective-permute-start.1
  696.4 10.1 %collective-permute-start.2 = (f32[512,128]{1,0:T(8,128)S(1)}, f32[512,128]{1,0:T(8,128)}, u32[]{:S(2)}, u32[]{:S(2)}) collective-permute-start(f32[512,128]{1,0:T(8,128)S(1)} %add.139), channel_id=1, source_target_pairs={{240,0},{0,16},{16,32},{32,48},{48,64},{64,80},{80,96},{96,112},{1... | collective-permute-start | bytes 786440 | tf_op jit(solution)/shard_map/while/body/eval_jaxpr/ppermute | solution.py:18
  710.0 12.5 %collective-permute-done.2 = f32[512,128]{1,0:T(8,128)} collective-permute-done((f32[512,128]{1,0:T(8,128)S(1)}, f32[512,128]{1,0:T(8,128)}, u32[]{:S(2)}, u32[]{:S(2)}) %collective-permute-start.2) | collective-permute-done | bytes 262176 | tf_op jit(solution)/shard_map/while/body/eval_jaxpr/ppermute | solution.py:18
  724.0 7.5 collective-permute-start
  733.1 6.3 collective-permute-start.1
  745.3 4.0 collective-permute-start.2
  752.8 11.1 %collective-permute-done.3 = f32[512,128]{1,0:T(8,128)} collective-permute-done((f32[512,128]{1,0:T(8,128)}, f32[512,128]{1,0:T(8,128)}, u32[]{:S(2)}, u32[]{:S(2)}) %collective-permute-start.3) | collective-permute-done | bytes 262176 | tf_op jit(solution)/shard_map/while/body/eval_jaxpr/ppermute | solution.py:18
  763.8 5.6 collective-permute-done.2
  778.5 4.3 all-to-all-start.8
  786.4 4.5 all-to-all-start.6
  792.7 11.8 %all-to-all-done.6 = bf16[4,128,1024]{2,1,0:T(8,128)(2,1)S(1)} async-done(((bf16[4,128,1024]{2,1,0:T(8,128)(2,1)}), bf16[4,128,1024]{2,1,0:T(8,128)(2,1)S(1)}, u32[]{:S(2)}, u32[]{:S(2)}) %all-to-all-start.6) | async-done | bytes 1048608 | tf_op jit(solution)/shard_map/all_to_all | solution.py:134
  (329 shorter events, 296.2 us)
Async XLA Ops:
  35.1 18.1 %all-to-all-start.2 = ((bf16[128,4,1024]{2,0,1:T(8,128)(2,1)}), bf16[128,4,1024]{2,0,1:T(8,128)(2,1)S(1)}, u32[]{:S(2)}, u32[]{:S(2)}) async-start(bf16[128,4,1024]{2,0,1:T(8,128)(2,1)} %bitcast.144), calls=%async_computation.2 | async-start | bytes 2097152 | tf_op jit(solution)/shard_map/all_to_all | solution.py:74
  53.2 18.8 %all-to-all-start.4 = ((bf16[128,4,1024]{2,0,1:T(8,128)(2,1)}), bf16[128,4,1024]{2,0,1:T(8,128)(2,1)}, u32[]{:S(2)}, u32[]{:S(2)}) async-start(bf16[128,4,1024]{2,0,1:T(8,128)(2,1)} %bitcast.143), calls=%async_computation.4 | async-start | bytes 2097152 | tf_op jit(solution)/shard_map/all_to_all | solution.py:75
  75.0 31.3 %collective-permute-start = (bf16[512,128]{0,1:T(8,128)(2,1)}, bf16[512,128]{0,1:T(8,128)(2,1)}, u32[]{:S(2)}, u32[]{:S(2)}) collective-permute-start(bf16[512,128]{0,1:T(8,128)(2,1)} %copy.118), channel_id=1, source_target_pairs={{0,16},{16,32},{32,48},{48,64},{64,80},{80,96},{96,112},{112,128},... | collective-permute-start | bytes 393224 | tf_op jit(solution)/shard_map/while/body/eval_jaxpr/ppermute | solution.py:12
  80.4 26.0 %collective-permute-start.1 = (bf16[512,128]{1,0:T(8,128)(2,1)}, bf16[512,128]{1,0:T(8,128)(2,1)}, u32[]{:S(2)}, u32[]{:S(2)}) collective-permute-start(bf16[512,128]{1,0:T(8,128)(2,1)} %copy.119), channel_id=1, source_target_pairs={{0,16},{16,32},{32,48},{48,64},{64,80},{80,96},{96,112},{112,128},... | collective-permute-start | bytes 393224 | tf_op jit(solution)/shard_map/while/body/eval_jaxpr/ppermute | solution.py:12
  102.9 15.9 %collective-permute-start.3 = (f32[512,128]{1,0:T(8,128)}, f32[512,128]{1,0:T(8,128)}, u32[]{:S(2)}, u32[]{:S(2)}) collective-permute-start(f32[512,128]{1,0:T(8,128)} %add.140), channel_id=1, source_target_pairs={{240,0},{0,16},{16,32},{32,48},{48,64},{64,80},{80,96},{96,112},{1... | collective-permute-start | bytes 786440 | tf_op jit(solution)/shard_map/while/body/eval_jaxpr/ppermute | solution.py:18
  104.4 25.9 %collective-permute-start.2 = (f32[512,128]{1,0:T(8,128)S(1)}, f32[512,128]{1,0:T(8,128)}, u32[]{:S(2)}, u32[]{:S(2)}) collective-permute-start(f32[512,128]{1,0:T(8,128)S(1)} %add.139), channel_id=1, source_target_pairs={{240,0},{0,16},{16,32},{32,48},{48,64},{64,80},{80,96},{96,112},{1... | collective-permute-start | bytes 786440 | tf_op jit(solution)/shard_map/while/body/eval_jaxpr/ppermute | solution.py:18
  131.9 27.3 %collective-permute-start = (bf16[512,128]{0,1:T(8,128)(2,1)}, bf16[512,128]{0,1:T(8,128)(2,1)}, u32[]{:S(2)}, u32[]{:S(2)}) collective-permute-start(bf16[512,128]{0,1:T(8,128)(2,1)} %copy.118), channel_id=1, source_target_pairs={{0,16},{16,32},{32,48},{48,64},{64,80},{80,96},{96,112},{112,128},... | collective-permute-start | bytes 393224 | tf_op jit(solution)/shard_map/while/body/eval_jaxpr/ppermute | solution.py:12
  135.4 23.8 %collective-permute-start.1 = (bf16[512,128]{1,0:T(8,128)(2,1)}, bf16[512,128]{1,0:T(8,128)(2,1)}, u32[]{:S(2)}, u32[]{:S(2)}) collective-permute-start(bf16[512,128]{1,0:T(8,128)(2,1)} %copy.119), channel_id=1, source_target_pairs={{0,16},{16,32},{32,48},{48,64},{64,80},{80,96},{96,112},{112,128},... | collective-permute-start | bytes 393224 | tf_op jit(solution)/shard_map/while/body/eval_jaxpr/ppermute | solution.py:12
  141.7 17.5 %collective-permute-start.3 = (f32[512,128]{1,0:T(8,128)}, f32[512,128]{1,0:T(8,128)}, u32[]{:S(2)}, u32[]{:S(2)}) collective-permute-start(f32[512,128]{1,0:T(8,128)} %add.140), channel_id=1, source_target_pairs={{240,0},{0,16},{16,32},{32,48},{48,64},{64,80},{80,96},{96,112},{1... | collective-permute-start | bytes 786440 | tf_op jit(solution)/shard_map/while/body/eval_jaxpr/ppermute | solution.py:18
  150.3 18.0 %collective-permute-start.2 = (f32[512,128]{1,0:T(8,128)S(1)}, f32[512,128]{1,0:T(8,128)}, u32[]{:S(2)}, u32[]{:S(2)}) collective-permute-start(f32[512,128]{1,0:T(8,128)S(1)} %add.139), channel_id=1, source_target_pairs={{240,0},{0,16},{16,32},{32,48},{48,64},{64,80},{80,96},{96,112},{1... | collective-permute-start | bytes 786440 | tf_op jit(solution)/shard_map/while/body/eval_jaxpr/ppermute | solution.py:18
  169.8 28.8 %collective-permute-start = (bf16[512,128]{0,1:T(8,128)(2,1)}, bf16[512,128]{0,1:T(8,128)(2,1)}, u32[]{:S(2)}, u32[]{:S(2)}) collective-permute-start(bf16[512,128]{0,1:T(8,128)(2,1)} %copy.118), channel_id=1, source_target_pairs={{0,16},{16,32},{32,48},{48,64},{64,80},{80,96},{96,112},{112,128},... | collective-permute-start | bytes 393224 | tf_op jit(solution)/shard_map/while/body/eval_jaxpr/ppermute | solution.py:12
  173.3 25.3 %collective-permute-start.1 = (bf16[512,128]{1,0:T(8,128)(2,1)}, bf16[512,128]{1,0:T(8,128)(2,1)}, u32[]{:S(2)}, u32[]{:S(2)}) collective-permute-start(bf16[512,128]{1,0:T(8,128)(2,1)} %copy.119), channel_id=1, source_target_pairs={{0,16},{16,32},{32,48},{48,64},{64,80},{80,96},{96,112},{112,128},... | collective-permute-start | bytes 393224 | tf_op jit(solution)/shard_map/while/body/eval_jaxpr/ppermute | solution.py:12
  182.7 15.9 %collective-permute-start.3 = (f32[512,128]{1,0:T(8,128)}, f32[512,128]{1,0:T(8,128)}, u32[]{:S(2)}, u32[]{:S(2)}) collective-permute-start(f32[512,128]{1,0:T(8,128)} %add.140), channel_id=1, source_target_pairs={{240,0},{0,16},{16,32},{32,48},{48,64},{64,80},{80,96},{96,112},{1... | collective-permute-start | bytes 786440 | tf_op jit(solution)/shard_map/while/body/eval_jaxpr/ppermute | solution.py:18
  183.7 19.2 %collective-permute-start.2 = (f32[512,128]{1,0:T(8,128)S(1)}, f32[512,128]{1,0:T(8,128)}, u32[]{:S(2)}, u32[]{:S(2)}) collective-permute-start(f32[512,128]{1,0:T(8,128)S(1)} %add.139), channel_id=1, source_target_pairs={{240,0},{0,16},{16,32},{32,48},{48,64},{64,80},{80,96},{96,112},{1... | collective-permute-start | bytes 786440 | tf_op jit(solution)/shard_map/while/body/eval_jaxpr/ppermute | solution.py:18
  204.5 25.6 %collective-permute-start = (bf16[512,128]{0,1:T(8,128)(2,1)}, bf16[512,128]{0,1:T(8,128)(2,1)}, u32[]{:S(2)}, u32[]{:S(2)}) collective-permute-start(bf16[512,128]{0,1:T(8,128)(2,1)} %copy.118), channel_id=1, source_target_pairs={{0,16},{16,32},{32,48},{48,64},{64,80},{80,96},{96,112},{112,128},... | collective-permute-start | bytes 393224 | tf_op jit(solution)/shard_map/while/body/eval_jaxpr/ppermute | solution.py:12
  211.8 18.2 %collective-permute-start.1 = (bf16[512,128]{1,0:T(8,128)(2,1)}, bf16[512,128]{1,0:T(8,128)(2,1)}, u32[]{:S(2)}, u32[]{:S(2)}) collective-permute-start(bf16[512,128]{1,0:T(8,128)(2,1)} %copy.119), channel_id=1, source_target_pairs={{0,16},{16,32},{32,48},{48,64},{64,80},{80,96},{96,112},{112,128},... | collective-permute-start | bytes 393224 | tf_op jit(solution)/shard_map/while/body/eval_jaxpr/ppermute | solution.py:12
  220.1 20.9 %collective-permute-start.3 = (f32[512,128]{1,0:T(8,128)}, f32[512,128]{1,0:T(8,128)}, u32[]{:S(2)}, u32[]{:S(2)}) collective-permute-start(f32[512,128]{1,0:T(8,128)} %add.140), channel_id=1, source_target_pairs={{240,0},{0,16},{16,32},{32,48},{48,64},{64,80},{80,96},{96,112},{1... | collective-permute-start | bytes 786440 | tf_op jit(solution)/shard_map/while/body/eval_jaxpr/ppermute | solution.py:18
  221.6 22.2 %collective-permute-start.2 = (f32[512,128]{1,0:T(8,128)S(1)}, f32[512,128]{1,0:T(8,128)}, u32[]{:S(2)}, u32[]{:S(2)}) collective-permute-start(f32[512,128]{1,0:T(8,128)S(1)} %add.139), channel_id=1, source_target_pairs={{240,0},{0,16},{16,32},{32,48},{48,64},{64,80},{80,96},{96,112},{1... | collective-permute-start | bytes 786440 | tf_op jit(solution)/shard_map/while/body/eval_jaxpr/ppermute | solution.py:18
  245.4 22.7 %collective-permute-start = (bf16[512,128]{0,1:T(8,128)(2,1)}, bf16[512,128]{0,1:T(8,128)(2,1)}, u32[]{:S(2)}, u32[]{:S(2)}) collective-permute-start(bf16[512,128]{0,1:T(8,128)(2,1)} %copy.118), channel_id=1, source_target_pairs={{0,16},{16,32},{32,48},{48,64},{64,80},{80,96},{96,112},{112,128},... | collective-permute-start | bytes 393224 | tf_op jit(solution)/shard_map/while/body/eval_jaxpr/ppermute | solution.py:12
  248.9 19.2 %collective-permute-start.1 = (bf16[512,128]{1,0:T(8,128)(2,1)}, bf16[512,128]{1,0:T(8,128)(2,1)}, u32[]{:S(2)}, u32[]{:S(2)}) collective-permute-start(bf16[512,128]{1,0:T(8,128)(2,1)} %copy.119), channel_id=1, source_target_pairs={{0,16},{16,32},{32,48},{48,64},{64,80},{80,96},{96,112},{112,128},... | collective-permute-start | bytes 393224 | tf_op jit(solution)/shard_map/while/body/eval_jaxpr/ppermute | solution.py:12
  255.2 37.3 %collective-permute-start.3 = (f32[512,128]{1,0:T(8,128)}, f32[512,128]{1,0:T(8,128)}, u32[]{:S(2)}, u32[]{:S(2)}) collective-permute-start(f32[512,128]{1,0:T(8,128)} %add.140), channel_id=1, source_target_pairs={{240,0},{0,16},{16,32},{32,48},{48,64},{64,80},{80,96},{96,112},{1... | collective-permute-start | bytes 786440 | tf_op jit(solution)/shard_map/while/body/eval_jaxpr/ppermute | solution.py:18
  256.6 42.2 %collective-permute-start.2 = (f32[512,128]{1,0:T(8,128)S(1)}, f32[512,128]{1,0:T(8,128)}, u32[]{:S(2)}, u32[]{:S(2)}) collective-permute-start(f32[512,128]{1,0:T(8,128)S(1)} %add.139), channel_id=1, source_target_pairs={{240,0},{0,16},{16,32},{32,48},{48,64},{64,80},{80,96},{96,112},{1... | collective-permute-start | bytes 786440 | tf_op jit(solution)/shard_map/while/body/eval_jaxpr/ppermute | solution.py:18
  300.3 14.4 %collective-permute-start = (bf16[512,128]{0,1:T(8,128)(2,1)}, bf16[512,128]{0,1:T(8,128)(2,1)}, u32[]{:S(2)}, u32[]{:S(2)}) collective-permute-start(bf16[512,128]{0,1:T(8,128)(2,1)} %copy.118), channel_id=1, source_target_pairs={{0,16},{16,32},{32,48},{48,64},{64,80},{80,96},{96,112},{112,128},... | collective-permute-start | bytes 393224 | tf_op jit(solution)/shard_map/while/body/eval_jaxpr/ppermute | solution.py:12
  310.2 15.0 %collective-permute-start.3 = (f32[512,128]{1,0:T(8,128)}, f32[512,128]{1,0:T(8,128)}, u32[]{:S(2)}, u32[]{:S(2)}) collective-permute-start(f32[512,128]{1,0:T(8,128)} %add.140), channel_id=1, source_target_pairs={{240,0},{0,16},{16,32},{32,48},{48,64},{64,80},{80,96},{96,112},{1... | collective-permute-start | bytes 786440 | tf_op jit(solution)/shard_map/while/body/eval_jaxpr/ppermute | solution.py:18
  311.2 17.9 %collective-permute-start.2 = (f32[512,128]{1,0:T(8,128)S(1)}, f32[512,128]{1,0:T(8,128)}, u32[]{:S(2)}, u32[]{:S(2)}) collective-permute-start(f32[512,128]{1,0:T(8,128)S(1)} %add.139), channel_id=1, source_target_pairs={{240,0},{0,16},{16,32},{32,48},{48,64},{64,80},{80,96},{96,112},{1... | collective-permute-start | bytes 786440 | tf_op jit(solution)/shard_map/while/body/eval_jaxpr/ppermute | solution.py:18
  330.6 33.4 %collective-permute-start = (bf16[512,128]{0,1:T(8,128)(2,1)}, bf16[512,128]{0,1:T(8,128)(2,1)}, u32[]{:S(2)}, u32[]{:S(2)}) collective-permute-start(bf16[512,128]{0,1:T(8,128)(2,1)} %copy.118), channel_id=1, source_target_pairs={{0,16},{16,32},{32,48},{48,64},{64,80},{80,96},{96,112},{112,128},... | collective-permute-start | bytes 393224 | tf_op jit(solution)/shard_map/while/body/eval_jaxpr/ppermute | solution.py:12
  337.7 26.4 %collective-permute-start.1 = (bf16[512,128]{1,0:T(8,128)(2,1)}, bf16[512,128]{1,0:T(8,128)(2,1)}, u32[]{:S(2)}, u32[]{:S(2)}) collective-permute-start(bf16[512,128]{1,0:T(8,128)(2,1)} %copy.119), channel_id=1, source_target_pairs={{0,16},{16,32},{32,48},{48,64},{64,80},{80,96},{96,112},{112,128},... | collective-permute-start | bytes 393224 | tf_op jit(solution)/shard_map/while/body/eval_jaxpr/ppermute | solution.py:12
  347.8 16.3 %collective-permute-start.3 = (f32[512,128]{1,0:T(8,128)}, f32[512,128]{1,0:T(8,128)}, u32[]{:S(2)}, u32[]{:S(2)}) collective-permute-start(f32[512,128]{1,0:T(8,128)} %add.140), channel_id=1, source_target_pairs={{240,0},{0,16},{16,32},{32,48},{48,64},{64,80},{80,96},{96,112},{1... | collective-permute-start | bytes 786440 | tf_op jit(solution)/shard_map/while/body/eval_jaxpr/ppermute | solution.py:18
  355.3 13.7 %collective-permute-start.2 = (f32[512,128]{1,0:T(8,128)S(1)}, f32[512,128]{1,0:T(8,128)}, u32[]{:S(2)}, u32[]{:S(2)}) collective-permute-start(f32[512,128]{1,0:T(8,128)S(1)} %add.139), channel_id=1, source_target_pairs={{240,0},{0,16},{16,32},{32,48},{48,64},{64,80},{80,96},{96,112},{1... | collective-permute-start | bytes 786440 | tf_op jit(solution)/shard_map/while/body/eval_jaxpr/ppermute | solution.py:18
  370.6 57.7 %collective-permute-start = (bf16[512,128]{0,1:T(8,128)(2,1)}, bf16[512,128]{0,1:T(8,128)(2,1)}, u32[]{:S(2)}, u32[]{:S(2)}) collective-permute-start(bf16[512,128]{0,1:T(8,128)(2,1)} %copy.118), channel_id=1, source_target_pairs={{0,16},{16,32},{32,48},{48,64},{64,80},{80,96},{96,112},{112,128},... | collective-permute-start | bytes 393224 | tf_op jit(solution)/shard_map/while/body/eval_jaxpr/ppermute | solution.py:12
  403.7 24.6 %collective-permute-start.1 = (bf16[512,128]{1,0:T(8,128)(2,1)}, bf16[512,128]{1,0:T(8,128)(2,1)}, u32[]{:S(2)}, u32[]{:S(2)}) collective-permute-start(bf16[512,128]{1,0:T(8,128)(2,1)} %copy.119), channel_id=1, source_target_pairs={{0,16},{16,32},{32,48},{48,64},{64,80},{80,96},{96,112},{112,128},... | collective-permute-start | bytes 393224 | tf_op jit(solution)/shard_map/while/body/eval_jaxpr/ppermute | solution.py:12
  419.7 13.0 %collective-permute-start.3 = (f32[512,128]{1,0:T(8,128)}, f32[512,128]{1,0:T(8,128)}, u32[]{:S(2)}, u32[]{:S(2)}) collective-permute-start(f32[512,128]{1,0:T(8,128)} %add.140), channel_id=1, source_target_pairs={{240,0},{0,16},{16,32},{32,48},{48,64},{64,80},{80,96},{96,112},{1... | collective-permute-start | bytes 786440 | tf_op jit(solution)/shard_map/while/body/eval_jaxpr/ppermute | solution.py:18
  423.3 20.6 %collective-permute-start.2 = (f32[512,128]{1,0:T(8,128)S(1)}, f32[512,128]{1,0:T(8,128)}, u32[]{:S(2)}, u32[]{:S(2)}) collective-permute-start(f32[512,128]{1,0:T(8,128)S(1)} %add.139), channel_id=1, source_target_pairs={{240,0},{0,16},{16,32},{32,48},{48,64},{64,80},{80,96},{96,112},{1... | collective-permute-start | bytes 786440 | tf_op jit(solution)/shard_map/while/body/eval_jaxpr/ppermute | solution.py:18
  445.4 23.1 %collective-permute-start = (bf16[512,128]{0,1:T(8,128)(2,1)}, bf16[512,128]{0,1:T(8,128)(2,1)}, u32[]{:S(2)}, u32[]{:S(2)}) collective-permute-start(bf16[512,128]{0,1:T(8,128)(2,1)} %copy.118), channel_id=1, source_target_pairs={{0,16},{16,32},{32,48},{48,64},{64,80},{80,96},{96,112},{112,128},... | collective-permute-start | bytes 393224 | tf_op jit(solution)/shard_map/while/body/eval_jaxpr/ppermute | solution.py:12
  448.9 19.6 %collective-permute-start.1 = (bf16[512,128]{1,0:T(8,128)(2,1)}, bf16[512,128]{1,0:T(8,128)(2,1)}, u32[]{:S(2)}, u32[]{:S(2)}) collective-permute-start(bf16[512,128]{1,0:T(8,128)(2,1)} %copy.119), channel_id=1, source_target_pairs={{0,16},{16,32},{32,48},{48,64},{64,80},{80,96},{96,112},{112,128},... | collective-permute-start | bytes 393224 | tf_op jit(solution)/shard_map/while/body/eval_jaxpr/ppermute | solution.py:12
  458.4 12.8 %collective-permute-start.3 = (f32[512,128]{1,0:T(8,128)}, f32[512,128]{1,0:T(8,128)}, u32[]{:S(2)}, u32[]{:S(2)}) collective-permute-start(f32[512,128]{1,0:T(8,128)} %add.140), channel_id=1, source_target_pairs={{240,0},{0,16},{16,32},{32,48},{48,64},{64,80},{80,96},{96,112},{1... | collective-permute-start | bytes 786440 | tf_op jit(solution)/shard_map/while/body/eval_jaxpr/ppermute | solution.py:18
  461.5 22.0 %collective-permute-start.2 = (f32[512,128]{1,0:T(8,128)S(1)}, f32[512,128]{1,0:T(8,128)}, u32[]{:S(2)}, u32[]{:S(2)}) collective-permute-start(f32[512,128]{1,0:T(8,128)S(1)} %add.139), channel_id=1, source_target_pairs={{240,0},{0,16},{16,32},{32,48},{48,64},{64,80},{80,96},{96,112},{1... | collective-permute-start | bytes 786440 | tf_op jit(solution)/shard_map/while/body/eval_jaxpr/ppermute | solution.py:18
  485.2 24.2 %collective-permute-start = (bf16[512,128]{0,1:T(8,128)(2,1)}, bf16[512,128]{0,1:T(8,128)(2,1)}, u32[]{:S(2)}, u32[]{:S(2)}) collective-permute-start(bf16[512,128]{0,1:T(8,128)(2,1)} %copy.118), channel_id=1, source_target_pairs={{0,16},{16,32},{32,48},{48,64},{64,80},{80,96},{96,112},{112,128},... | collective-permute-start | bytes 393224 | tf_op jit(solution)/shard_map/while/body/eval_jaxpr/ppermute | solution.py:12
  492.5 16.9 %collective-permute-start.1 = (bf16[512,128]{1,0:T(8,128)(2,1)}, bf16[512,128]{1,0:T(8,128)(2,1)}, u32[]{:S(2)}, u32[]{:S(2)}) collective-permute-start(bf16[512,128]{1,0:T(8,128)(2,1)} %copy.119), channel_id=1, source_target_pairs={{0,16},{16,32},{32,48},{48,64},{64,80},{80,96},{96,112},{112,128},... | collective-permute-start | bytes 393224 | tf_op jit(solution)/shard_map/while/body/eval_jaxpr/ppermute | solution.py:12
  503.9 13.5 %collective-permute-start.2 = (f32[512,128]{1,0:T(8,128)S(1)}, f32[512,128]{1,0:T(8,128)}, u32[]{:S(2)}, u32[]{:S(2)}) collective-permute-start(f32[512,128]{1,0:T(8,128)S(1)} %add.139), channel_id=1, source_target_pairs={{240,0},{0,16},{16,32},{32,48},{48,64},{64,80},{80,96},{96,112},{1... | collective-permute-start | bytes 786440 | tf_op jit(solution)/shard_map/while/body/eval_jaxpr/ppermute | solution.py:18
  519.0 19.6 %collective-permute-start = (bf16[512,128]{0,1:T(8,128)(2,1)}, bf16[512,128]{0,1:T(8,128)(2,1)}, u32[]{:S(2)}, u32[]{:S(2)}) collective-permute-start(bf16[512,128]{0,1:T(8,128)(2,1)} %copy.118), channel_id=1, source_target_pairs={{0,16},{16,32},{32,48},{48,64},{64,80},{80,96},{96,112},{112,128},... | collective-permute-start | bytes 393224 | tf_op jit(solution)/shard_map/while/body/eval_jaxpr/ppermute | solution.py:12
  526.5 12.1 %collective-permute-start.1 = (bf16[512,128]{1,0:T(8,128)(2,1)}, bf16[512,128]{1,0:T(8,128)(2,1)}, u32[]{:S(2)}, u32[]{:S(2)}) collective-permute-start(bf16[512,128]{1,0:T(8,128)(2,1)} %copy.119), channel_id=1, source_target_pairs={{0,16},{16,32},{32,48},{48,64},{64,80},{80,96},{96,112},{112,128},... | collective-permute-start | bytes 393224 | tf_op jit(solution)/shard_map/while/body/eval_jaxpr/ppermute | solution.py:12
  534.1 11.4 %collective-permute-start.3 = (f32[512,128]{1,0:T(8,128)}, f32[512,128]{1,0:T(8,128)}, u32[]{:S(2)}, u32[]{:S(2)}) collective-permute-start(f32[512,128]{1,0:T(8,128)} %add.140), channel_id=1, source_target_pairs={{240,0},{0,16},{16,32},{32,48},{48,64},{64,80},{80,96},{96,112},{1... | collective-permute-start | bytes 786440 | tf_op jit(solution)/shard_map/while/body/eval_jaxpr/ppermute | solution.py:18
  535.1 13.2 %collective-permute-start.2 = (f32[512,128]{1,0:T(8,128)S(1)}, f32[512,128]{1,0:T(8,128)}, u32[]{:S(2)}, u32[]{:S(2)}) collective-permute-start(f32[512,128]{1,0:T(8,128)S(1)} %add.139), channel_id=1, source_target_pairs={{240,0},{0,16},{16,32},{32,48},{48,64},{64,80},{80,96},{96,112},{1... | collective-permute-start | bytes 786440 | tf_op jit(solution)/shard_map/while/body/eval_jaxpr/ppermute | solution.py:18
  549.9 22.4 %collective-permute-start = (bf16[512,128]{0,1:T(8,128)(2,1)}, bf16[512,128]{0,1:T(8,128)(2,1)}, u32[]{:S(2)}, u32[]{:S(2)}) collective-permute-start(bf16[512,128]{0,1:T(8,128)(2,1)} %copy.118), channel_id=1, source_target_pairs={{0,16},{16,32},{32,48},{48,64},{64,80},{80,96},{96,112},{112,128},... | collective-permute-start | bytes 393224 | tf_op jit(solution)/shard_map/while/body/eval_jaxpr/ppermute | solution.py:12
  553.4 18.9 %collective-permute-start.1 = (bf16[512,128]{1,0:T(8,128)(2,1)}, bf16[512,128]{1,0:T(8,128)(2,1)}, u32[]{:S(2)}, u32[]{:S(2)}) collective-permute-start(bf16[512,128]{1,0:T(8,128)(2,1)} %copy.119), channel_id=1, source_target_pairs={{0,16},{16,32},{32,48},{48,64},{64,80},{80,96},{96,112},{112,128},... | collective-permute-start | bytes 393224 | tf_op jit(solution)/shard_map/while/body/eval_jaxpr/ppermute | solution.py:12
  563.5 17.6 %collective-permute-start.2 = (f32[512,128]{1,0:T(8,128)S(1)}, f32[512,128]{1,0:T(8,128)}, u32[]{:S(2)}, u32[]{:S(2)}) collective-permute-start(f32[512,128]{1,0:T(8,128)S(1)} %add.139), channel_id=1, source_target_pairs={{240,0},{0,16},{16,32},{32,48},{48,64},{64,80},{80,96},{96,112},{1... | collective-permute-start | bytes 786440 | tf_op jit(solution)/shard_map/while/body/eval_jaxpr/ppermute | solution.py:18
  582.6 31.0 %collective-permute-start = (bf16[512,128]{0,1:T(8,128)(2,1)}, bf16[512,128]{0,1:T(8,128)(2,1)}, u32[]{:S(2)}, u32[]{:S(2)}) collective-permute-start(bf16[512,128]{0,1:T(8,128)(2,1)} %copy.118), channel_id=1, source_target_pairs={{0,16},{16,32},{32,48},{48,64},{64,80},{80,96},{96,112},{112,128},... | collective-permute-start | bytes 393224 | tf_op jit(solution)/shard_map/while/body/eval_jaxpr/ppermute | solution.py:12
  586.1 27.5 %collective-permute-start.1 = (bf16[512,128]{1,0:T(8,128)(2,1)}, bf16[512,128]{1,0:T(8,128)(2,1)}, u32[]{:S(2)}, u32[]{:S(2)}) collective-permute-start(bf16[512,128]{1,0:T(8,128)(2,1)} %copy.119), channel_id=1, source_target_pairs={{0,16},{16,32},{32,48},{48,64},{64,80},{80,96},{96,112},{112,128},... | collective-permute-start | bytes 393224 | tf_op jit(solution)/shard_map/while/body/eval_jaxpr/ppermute | solution.py:12
  594.0 19.6 %collective-permute-start.3 = (f32[512,128]{1,0:T(8,128)}, f32[512,128]{1,0:T(8,128)}, u32[]{:S(2)}, u32[]{:S(2)}) collective-permute-start(f32[512,128]{1,0:T(8,128)} %add.140), channel_id=1, source_target_pairs={{240,0},{0,16},{16,32},{32,48},{48,64},{64,80},{80,96},{96,112},{1... | collective-permute-start | bytes 786440 | tf_op jit(solution)/shard_map/while/body/eval_jaxpr/ppermute | solution.py:18
  600.0 14.9 %collective-permute-start.2 = (f32[512,128]{1,0:T(8,128)S(1)}, f32[512,128]{1,0:T(8,128)}, u32[]{:S(2)}, u32[]{:S(2)}) collective-permute-start(f32[512,128]{1,0:T(8,128)S(1)} %add.139), channel_id=1, source_target_pairs={{240,0},{0,16},{16,32},{32,48},{48,64},{64,80},{80,96},{96,112},{1... | collective-permute-start | bytes 786440 | tf_op jit(solution)/shard_map/while/body/eval_jaxpr/ppermute | solution.py:18
  616.5 44.2 %collective-permute-start = (bf16[512,128]{0,1:T(8,128)(2,1)}, bf16[512,128]{0,1:T(8,128)(2,1)}, u32[]{:S(2)}, u32[]{:S(2)}) collective-permute-start(bf16[512,128]{0,1:T(8,128)(2,1)} %copy.118), channel_id=1, source_target_pairs={{0,16},{16,32},{32,48},{48,64},{64,80},{80,96},{96,112},{112,128},... | collective-permute-start | bytes 393224 | tf_op jit(solution)/shard_map/while/body/eval_jaxpr/ppermute | solution.py:12
  623.9 36.8 %collective-permute-start.1 = (bf16[512,128]{1,0:T(8,128)(2,1)}, bf16[512,128]{1,0:T(8,128)(2,1)}, u32[]{:S(2)}, u32[]{:S(2)}) collective-permute-start(bf16[512,128]{1,0:T(8,128)(2,1)} %copy.119), channel_id=1, source_target_pairs={{0,16},{16,32},{32,48},{48,64},{64,80},{80,96},{96,112},{112,128},... | collective-permute-start | bytes 393224 | tf_op jit(solution)/shard_map/while/body/eval_jaxpr/ppermute | solution.py:12
  641.5 19.2 %collective-permute-start.3 = (f32[512,128]{1,0:T(8,128)}, f32[512,128]{1,0:T(8,128)}, u32[]{:S(2)}, u32[]{:S(2)}) collective-permute-start(f32[512,128]{1,0:T(8,128)} %add.140), channel_id=1, source_target_pairs={{240,0},{0,16},{16,32},{32,48},{48,64},{64,80},{80,96},{96,112},{1... | collective-permute-start | bytes 786440 | tf_op jit(solution)/shard_map/while/body/eval_jaxpr/ppermute | solution.py:18
  645.1 20.6 %collective-permute-start.2 = (f32[512,128]{1,0:T(8,128)S(1)}, f32[512,128]{1,0:T(8,128)}, u32[]{:S(2)}, u32[]{:S(2)}) collective-permute-start(f32[512,128]{1,0:T(8,128)S(1)} %add.139), channel_id=1, source_target_pairs={{240,0},{0,16},{16,32},{32,48},{48,64},{64,80},{80,96},{96,112},{1... | collective-permute-start | bytes 786440 | tf_op jit(solution)/shard_map/while/body/eval_jaxpr/ppermute | solution.py:18
  667.3 42.7 %collective-permute-start = (bf16[512,128]{0,1:T(8,128)(2,1)}, bf16[512,128]{0,1:T(8,128)(2,1)}, u32[]{:S(2)}, u32[]{:S(2)}) collective-permute-start(bf16[512,128]{0,1:T(8,128)(2,1)} %copy.118), channel_id=1, source_target_pairs={{0,16},{16,32},{32,48},{48,64},{64,80},{80,96},{96,112},{112,128},... | collective-permute-start | bytes 393224 | tf_op jit(solution)/shard_map/while/body/eval_jaxpr/ppermute | solution.py:12
  684.2 25.7 %collective-permute-start.1 = (bf16[512,128]{1,0:T(8,128)(2,1)}, bf16[512,128]{1,0:T(8,128)(2,1)}, u32[]{:S(2)}, u32[]{:S(2)}) collective-permute-start(bf16[512,128]{1,0:T(8,128)(2,1)} %copy.119), channel_id=1, source_target_pairs={{0,16},{16,32},{32,48},{48,64},{64,80},{80,96},{96,112},{112,128},... | collective-permute-start | bytes 393224 | tf_op jit(solution)/shard_map/while/body/eval_jaxpr/ppermute | solution.py:12
  694.9 15.0 %collective-permute-start.3 = (f32[512,128]{1,0:T(8,128)}, f32[512,128]{1,0:T(8,128)}, u32[]{:S(2)}, u32[]{:S(2)}) collective-permute-start(f32[512,128]{1,0:T(8,128)} %add.140), channel_id=1, source_target_pairs={{240,0},{0,16},{16,32},{32,48},{48,64},{64,80},{80,96},{96,112},{1... | collective-permute-start | bytes 786440 | tf_op jit(solution)/shard_map/while/body/eval_jaxpr/ppermute | solution.py:18
  696.4 26.0 %collective-permute-start.2 = (f32[512,128]{1,0:T(8,128)S(1)}, f32[512,128]{1,0:T(8,128)}, u32[]{:S(2)}, u32[]{:S(2)}) collective-permute-start(f32[512,128]{1,0:T(8,128)S(1)} %add.139), channel_id=1, source_target_pairs={{240,0},{0,16},{16,32},{32,48},{48,64},{64,80},{80,96},{96,112},{1... | collective-permute-start | bytes 786440 | tf_op jit(solution)/shard_map/while/body/eval_jaxpr/ppermute | solution.py:18
  724.0 28.8 %collective-permute-start = (bf16[512,128]{0,1:T(8,128)(2,1)}, bf16[512,128]{0,1:T(8,128)(2,1)}, u32[]{:S(2)}, u32[]{:S(2)}) collective-permute-start(bf16[512,128]{0,1:T(8,128)(2,1)} %copy.118), channel_id=1, source_target_pairs={{0,16},{16,32},{32,48},{48,64},{64,80},{80,96},{96,112},{112,128},... | collective-permute-start | bytes 393224 | tf_op jit(solution)/shard_map/while/body/eval_jaxpr/ppermute | solution.py:12
  733.1 19.7 %collective-permute-start.1 = (bf16[512,128]{1,0:T(8,128)(2,1)}, bf16[512,128]{1,0:T(8,128)(2,1)}, u32[]{:S(2)}, u32[]{:S(2)}) collective-permute-start(bf16[512,128]{1,0:T(8,128)(2,1)} %copy.119), channel_id=1, source_target_pairs={{0,16},{16,32},{32,48},{48,64},{64,80},{80,96},{96,112},{112,128},... | collective-permute-start | bytes 393224 | tf_op jit(solution)/shard_map/while/body/eval_jaxpr/ppermute | solution.py:12
  743.8 20.0 %collective-permute-start.3 = (f32[512,128]{1,0:T(8,128)}, f32[512,128]{1,0:T(8,128)}, u32[]{:S(2)}, u32[]{:S(2)}) collective-permute-start(f32[512,128]{1,0:T(8,128)} %add.140), channel_id=1, source_target_pairs={{240,0},{0,16},{16,32},{32,48},{48,64},{64,80},{80,96},{96,112},{1... | collective-permute-start | bytes 786440 | tf_op jit(solution)/shard_map/while/body/eval_jaxpr/ppermute | solution.py:18
  745.3 24.1 %collective-permute-start.2 = (f32[512,128]{1,0:T(8,128)S(1)}, f32[512,128]{1,0:T(8,128)}, u32[]{:S(2)}, u32[]{:S(2)}) collective-permute-start(f32[512,128]{1,0:T(8,128)S(1)} %add.139), channel_id=1, source_target_pairs={{240,0},{0,16},{16,32},{32,48},{48,64},{64,80},{80,96},{96,112},{1... | collective-permute-start | bytes 786440 | tf_op jit(solution)/shard_map/while/body/eval_jaxpr/ppermute | solution.py:18
  786.4 18.1 %all-to-all-start.6 = ((bf16[4,128,1024]{2,1,0:T(8,128)(2,1)}), bf16[4,128,1024]{2,1,0:T(8,128)(2,1)S(1)}, u32[]{:S(2)}, u32[]{:S(2)}) async-start(bf16[4,128,1024]{2,1,0:T(8,128)(2,1)} %bitcast.38), calls=%async_computation.6 | async-start | bytes 2097152 | tf_op jit(solution)/shard_map/all_to_all | solution.py:134
  (14 other events, 160.8 us)
where the time goes:
time: 819 us; the launch traced here: 806 us
  starting transfers between devices  344 us (42%)
  waiting for transfers between devices  240 us (29%)
  other arithmetic  132 us (16%)
  local copies, waits for them, and re-layouts  67.8 us (8%)
  matrix products  12.2 us (1%)
  loops' own time  10.8 us (1%)
    ppermute x32, waiting for transfers between devices, from_behind_2(): return lax.ppermute(block, axis, route)  194 us
    ppermute x32, starting transfers between devices, from_behind(): return lax.ppermute(array, axis, pairs)  186 us
    ppermute x32, starting transfers between devices, from_behind_2(): return lax.ppermute(block, axis, route)  115 us
    add x16, other arithmetic, travel_turn(): return (key_cur, value_cur, key_acc, value_acc, query_acc + query_term)  53.1 us
    while x32, local copies, waits for them, and re-layouts  50.1 us
    add x16, other arithmetic, travel_turn(): value_acc + value_term  26.9 us
    reduce_or x16, other arithmetic, visit(): return lax.cond(jnp.any(allowed), compute_terms, empty_terms)  26.8 us
  transfers between devices with their start and end apart: 73, of which 34 were waited for; matrix products, arithmetic and copies ran while one was open for 23% of the time, Pallas kernels for 0%

commit v1 on v0

v1 whole, which is shorter than its diff:
```python
import functools

import jax
import jax.numpy as jnp
from jax import lax
from jax.experimental import pallas as pl
from jax.experimental.pallas import tpu as pltpu
from jax.sharding import PartitionSpec as P

HD = 128
LOG2E = 1.4426950408889634
SCALE = HD ** (-0.5)
HOPS = 8
MASKED = -1e30
MESH = pl.DeviceIdType.MESH
NN = (((1,), (0,)), ((), ()))
NT = (((1,), (1,)), ((), ()))
BF = jnp.bfloat16
F32 = jnp.float32


def dot(a, b, dims):
    return lax.dot_general(a, b, dims, preferred_element_type=F32)


def kernel(
    chips, group, rows, parts,
    q_hbm, k_hbm, v_hbm, o_hbm, do_hbm, lse_ref, len_ref,
    dq_hbm, dk_ref, dv_ref,
    qs, dos, qt, dot_t, o_nat, do_nat, lb, db, lo_ref, pd, dqacc, dqs,
    kv, acc, pf, p8, own, h8, home,
    fh_send, fh_recv, ring_send, ring_recv, acc_send, acc_recv,
    home_send, home_recv, h8_send, h8_recv, own_send, own_recv,
    nat_sem, q_loc, q_send, q_recv, pd_send, pd_recv, dq_loc, dq_send, dq_recv,
):
    heads = 2 * group
    block = 2 * rows
    at_ctx, at_head = lax.axis_index("ctx"), lax.axis_index("head")
    core = lax.rem(at_head, 2)
    chip = at_ctx * 2 + lax.div(at_head, 2)
    other = 1 - core

    def device(hop, to_core):
        to = lax.rem(chip + hop + chips, chips)
        return {"ctx": lax.div(to, 2), "head": lax.rem(to, 2) * 2 + to_core}

    def remote(src, dst, ss, rs, hop, to_core):
        return pltpu.make_async_remote_copy(
            src_ref=src, dst_ref=dst, send_sem=ss, recv_sem=rs,
            device_id=device(hop, to_core), device_id_type=MESH,
        )

    def cols(head, width=1):
        return pl.ds(pl.multiple_of(head * HD, HD), width * HD)

    def half(which):
        return pl.ds(pl.multiple_of(which * rows, rows), rows)

    barrier = pltpu.get_barrier_semaphore()
    partners = [(0, other)] + [(h, c) for h in (1, -1, 7, -7, 8, -8) for c in (0, 1)]
    for hop, c in partners:
        pl.semaphore_signal(barrier, inc=1, device_id=device(hop, c), device_id_type=MESH)
    nat = [
        pltpu.make_async_copy(o_hbm, o_nat, nat_sem.at[0]),
        pltpu.make_async_copy(do_hbm, do_nat, nat_sem.at[1]),
    ]
    for cp in nat:
        cp.start()
    pl.semaphore_wait(barrier, len(partners))

    kinds = [(0, 0, 1, 1), (1, 1, 1, 7), (2, 0, 0, 0), (3, 1, 8, 0), (4, 0, 8, 8), (5, 1, 0, 8)]

    def first(kind, d, which):
        _, b, slot, hop = kinds[kind]
        to_core = core if d == 0 else other
        src = (k_hbm, v_hbm)[which].at[:, cols(2 * to_core + b)]
        dst = kv.at[b, slot, which, half(core)]
        if hop == 0 and d == 0:
            return pltpu.make_async_copy(src, dst, fh_recv.at[kind, core, which])
        return remote(src, dst, fh_send.at[kind, d, which], fh_recv.at[kind, core, which], hop, to_core)

    def start_first(kind):
        for which in (0, 1):
            for d in (0, 1):
                first(kind, d, which).start()

    def wait_first(kind, which):
        _, b, slot, hop = kinds[kind]
        for c in (0, 1):
            dst = kv.at[b, slot, which, pl.ds(c * rows, rows)]
            pltpu.make_async_copy(dst, dst, fh_recv.at[kind, c, which]).wait()

    start_first(0)
    start_first(1)

    @pl.loop(0, heads)
    def _(h):
        for i, (src, dst) in enumerate(((q_hbm, qs), (do_hbm, dos))):
            pltpu.make_async_copy(
                src.at[:, cols(heads * core + h)], dst.at[h, half(core)], q_loc.at[i]
            ).start()
            remote(
                src.at[:, cols(heads * other + h)], dst.at[h, half(core)],
                q_send.at[i], q_recv.at[i], 0, other,
            ).start()

    for kind in (2, 3, 5, 4):
        start_first(kind)

    for cp in nat:
        cp.wait()
    lane = lax.broadcasted_iota(jnp.int32, (rows, 4 * group), 1)
    delta = jnp.zeros((rows, 4 * group), F32)
    for h in range(4 * group):
        at = slice(h * HD, (h + 1) * HD)
        col = jnp.sum(o_nat[:, at].astype(F32) * do_nat[:, at].astype(F32), axis=1, keepdims=True)
        delta = jnp.where(lane == h, col, delta)
    norm = lse_ref[...] * LOG2E
    first_half = core == 0
    for i, flip in ((0, False), (1, True)):
        low = jnp.logical_xor(first_half, flip)
        pd[i, :, :heads] = jnp.where(low, norm[:, :heads], norm[:, heads:])
        pd[i, :, heads : 2 * heads] = jnp.where(low, delta[:, :heads], delta[:, heads:])
    pd_copy = remote(pd.at[1], pd.at[2], pd_send.at[0], pd_recv.at[0], 0, other)
    pd_copy.start()

    row = chip * block + lax.broadcasted_iota(jnp.int32, (block, HD), 0)
    low_key = jnp.zeros((block, HD), jnp.int32)
    end = jnp.int32(0)
    for d in range(len_ref.shape[0]):
        end = end + len_ref[d]
        low_key = jnp.where(row >= end, end, low_key)
    lo_ref[...] = low_key

    dqacc[...] = jnp.zeros_like(dqacc)
    for b in (0, 1):
        acc[b, 1] = jnp.zeros(acc.shape[2:], acc.dtype)

    for i, dst in enumerate((qs, dos)):
        mine = dst.at[:, half(core)]
        theirs = dst.at[:, half(other)]
        pltpu.make_async_copy(mine, mine, q_loc.at[i]).wait()
        pltpu.make_async_copy(theirs, theirs, q_recv.at[i]).wait()
    for h in range(heads):
        at = slice(h * block, (h + 1) * block)
        qt[:, at] = qs[h].T
        dot_t[:, at] = dos[h].T
    pd_copy.wait_recv()
    for i, at in ((0, core), (2, other)):
        for h in range(heads):
            lb[h, half(at)] = jnp.broadcast_to(pd[i, :, h : h + 1], (rows, HD))
            db[h, half(at)] = jnp.broadcast_to(pd[i, :, heads + h : heads + h + 1], (rows, HD))

    def ring(b, t, which):
        return remote(
            kv.at[b, t, which], kv.at[b, t + 1, which],
            ring_send.at[b, t, which], ring_recv.at[b, t + 1, which], 1 - 2 * b, core,
        )

    def pass_on(b, t, which):
        return remote(
            acc.at[b, t, which], acc.at[b, t + 1, which],
            acc_send.at[b, t, which], acc_recv.at[b, t + 1, which], 1 - 2 * b, core,
        )

    def go_home(b, which, r):
        return remote(
            acc.at[b, HOPS - 1, which, pl.ds(r * rows, rows)], home.at[b, core, which],
            home_send.at[b, r, which], home_recv.at[b, core, which], -7 if b == 0 else -1, r,
        )

    def far_home(b, which, r):
        return remote(
            p8.at[b, which, pl.ds(r * rows, rows)], h8.at[b, core, which],
            h8_send.at[b, r, which], h8_recv.at[b, core, which], -8, r,
        )

    def own_home(b, which):
        return remote(
            pf.at[b, which, half(other)], own.at[b, core, which],
            own_send.at[b, which], own_recv.at[b, which], 0, other,
        )

    def chunk(b, slot, distance):
        keys = kv[b, slot, 0]
        values = kv[b, slot, 1]
        key_at = (chip - distance) * block + lax.broadcasted_iota(jnp.int32, (block, block), 1)
        row_at = chip * block + lax.broadcasted_iota(jnp.int32, (block, block), 0)
        low = jnp.concatenate([lo_ref[...]] * (block // HD), axis=1) if block >= HD else lo_ref[:, :block]
        bias = jnp.where((key_at >= low) & (key_at <= row_at), 0.0, MASKED)
        dk_t = jnp.zeros((HD, block), F32)
        dv_t = jnp.zeros((HD, block), F32)
        step = min(4, group)
        for h in range(b * group, (b + 1) * group, step):
            some = slice(h, h + step)
            flat = slice(h * block, (h + step) * block)

            def wide(ref):
                x = ref[some]
                return jnp.concatenate([x] * (block // HD), axis=2) if block >= HD else x[:, :, :block]

            q = qs[some].reshape(step * block, HD)
            g = dos[some].reshape(step * block, HD)
            s = dot(q, keys, NT).reshape(step, block, block)
            dp = dot(g, values, NT).reshape(step, block, block)
            p = jnp.exp2(s * (SCALE * LOG2E) - wide(lb) + bias[None])
            ds = (p * (dp - wide(db))).astype(BF).reshape(step * block, block)
            ph = p.astype(BF).reshape(step * block, block)
            dv_t = dv_t + dot(dot_t[:, flat], ph, NN)
            dk_t = dk_t + dot(qt[:, flat], ds, NN)
            dqacc[some] += dot(ds, keys, NN).reshape(step, block, HD)
        pf[b, 0] = dk_t.T
        pf[b, 1] = dv_t.T

    for which in (0, 1):
        for b in (0, 1):
            wait_first(b, which)
            ring(b, 1, which).start()

    for b in (0, 1):
        for which in (0, 1):
            wait_first(2 + b, which)
        chunk(b, HOPS * b, 0)
        for which in (0, 1):
            own_home(b, which).start()
            own[b, core, which] = pf[b, which, half(core)]
    for b in (0, 1):
        for which in (0, 1):
            own_home(b, which).wait_send()

    @pl.loop(1, HOPS)
    def _(t):
        chunk(0, t, t)
        chunk(1, t, HOPS - t)

        @pl.when(t < HOPS - 1)
        def _():
            for which in (0, 1):
                for b in (0, 1):
                    ring(b, t, which).wait_recv()

                    @pl.when(t + 1 < HOPS - 1)
                    def _():
                        ring(b, t + 1, which).start()

        for b in (0, 1):
            for which in (0, 1):
                @pl.when(t > 1)
                def _():
                    pass_on(b, t - 1, which).wait_recv()

                acc[b, t, which] = (acc[b, t, which].astype(F32) + pf[b, which]).astype(BF)

                @pl.when(t < HOPS - 1)
                def _():
                    pass_on(b, t, which).start()

                @pl.when(t == HOPS - 1)
                def _():
                    for r in (0, 1):
                        go_home(b, which, r).start()

        @pl.when(t == 2)
        def _():
            for b in (0, 1):
                for which in (0, 1):
                    wait_first(4 + b, which)
                chunk(b, HOPS * (1 - b), HOPS)
                for which in (0, 1):
                    p8[b, which] = pf[b, which].astype(BF)
                    for r in (0, 1):
                        far_home(b, which, r).start()

    dqs[...] = (dqacc[...] * SCALE).astype(BF)

    @pl.loop(0, heads)
    def _(h):
        pltpu.make_async_copy(
            dqs.at[h, half(core)], dq_hbm.at[:, cols(heads * core + h)], dq_loc.at[0]
        ).start()
        remote(
            dqs.at[h, half(other)], dq_hbm.at[:, cols(heads * core + h)],
            dq_send.at[0], dq_recv.at[0], 0, other,
        ).start()

    for b in (0, 1):
        for which in (0, 1):
            got = own.at[b, other, which]
            pltpu.make_async_copy(got, got, own_recv.at[b, which]).wait()
            for c in (0, 1):
                for buf, sems in ((h8, h8_recv), (home, home_recv)):
                    got = buf.at[b, c, which]
                    pltpu.make_async_copy(got, got, sems.at[b, c, which]).wait()
    for c in (0, 1):
        for b in (0, 1):
            at = slice((2 * c + b) * HD, (2 * c + b + 1) * HD)
            total = [
                own[b, c, which] + h8[b, c, which].astype(F32) + home[b, c, which].astype(F32)
                for which in (0, 1)
            ]
            dk_ref[:, at] = (total[0] * SCALE).astype(BF)
            dv_ref[:, at] = total[1].astype(BF)

    for i, dst in enumerate((qs, dos)):
        out = dst.at[:, half(core)]
        pltpu.make_async_copy(out, out, q_send.at[i]).wait()
    pd_copy.wait_send()
    for kind in range(6):
        for which in (0, 1):
            for d in (0, 1):
                if not (kinds[kind][3] == 0 and d == 0):
                    first(kind, d, which).wait_send()
    for b in (0, 1):
        for which in (0, 1):
            for r in (0, 1):
                far_home(b, which, r).wait_send()
                go_home(b, which, r).wait_send()
            for t in range(1, HOPS - 1):
                ring(b, t, which).wait_send()
                pass_on(b, t, which).wait_send()
    out = dq_hbm.at[:, cols(heads * core, heads)]
    pltpu.make_async_copy(out, out, dq_loc.at[0]).wait()
    pltpu.make_async_copy(out, out, dq_send.at[0]).wait()
    got = dq_hbm.at[:, cols(heads * other, heads)]
    pltpu.make_async_copy(got, got, dq_recv.at[0]).wait()


def body(query_rows, key_rows, value_rows, fwd_output, grad_output, log_normalizer, doc_lengths):
    rows = query_rows.shape[0]
    group = query_rows.shape[1] // key_rows.shape[1]
    chips = lax.axis_size("ctx") * 2
    heads = 2 * group
    block = 2 * rows
    any_space = pl.BlockSpec(memory_space=pl.ANY)
    vmem = pl.BlockSpec(memory_space=pltpu.VMEM)
    smem = pl.BlockSpec(memory_space=pltpu.SMEM)
    dma = pltpu.SemaphoreType.DMA
    slots = HOPS + 1
    flops = 2 * slots * group * block * block * HD * 2 * 5
    return pl.pallas_call(
        functools.partial(kernel, chips, group, rows, None),
        out_shape=[
            jax.ShapeDtypeStruct(query_rows.shape, BF),
            jax.ShapeDtypeStruct(key_rows.shape, BF),
            jax.ShapeDtypeStruct(value_rows.shape, BF),
        ],
        in_specs=[any_space] * 5 + [vmem, smem],
        out_specs=[any_space, vmem, vmem],
        scratch_shapes=[
            pltpu.VMEM((heads, block, HD), BF),
            pltpu.VMEM((heads, block, HD), BF),
            pltpu.VMEM((HD, heads * block), BF),
            pltpu.VMEM((HD, heads * block), BF),
            pltpu.VMEM((rows, 2 * heads * HD), BF),
            pltpu.VMEM((rows, 2 * heads * HD), BF),
            pltpu.VMEM((heads, block, HD), F32),
            pltpu.VMEM((heads, block, HD), F32),
            pltpu.VMEM((block, HD), jnp.int32),
            pltpu.VMEM((3, rows, HD), F32),
            pltpu.VMEM((heads, block, HD), F32),
            pltpu.VMEM((heads, block, HD), BF),
            pltpu.VMEM((2, slots, 2, block, HD), BF),
            pltpu.VMEM((2, HOPS, 2, block, HD), BF),
            pltpu.VMEM((2, 2, block, HD), F32),
            pltpu.VMEM((2, 2, block, HD), BF),
            pltpu.VMEM((2, 2, 2, rows, HD), F32),
            pltpu.VMEM((2, 2, 2, rows, HD), BF),
            pltpu.VMEM((2, 2, 2, rows, HD), BF),
            dma((6, 2, 2)), dma((6, 2, 2)),
            dma((2, slots, 2)), dma((2, slots, 2)),
            dma((2, slots, 2)), dma((2, slots, 2)),
            dma((2, 2, 2)), dma((2, 2, 2)),
            dma((2, 2, 2)), dma((2, 2, 2)),
            dma((2, 2)), dma((2, 2)),
            dma((2,)), dma((2,)), dma((2,)), dma((2,)),
            dma((1,)), dma((1,)), dma((1,)), dma((1,)), dma((1,)),
        ],
        compiler_params=pltpu.CompilerParams(
            collective_id=0, has_side_effects=True, vmem_limit_bytes=56 * 2**20
        ),
        cost_estimate=pl.CostEstimate(
            flops=flops, bytes_accessed=8 * rows * 2 * heads * HD, transcendentals=flops // (10 * HD)
        ),
    )(query_rows, key_rows, value_rows, fwd_output, grad_output, log_normalizer, doc_lengths)


def solution(mesh):
    tokens = P(("dp", "ctx", "head"), None)
    return jax.shard_map(
        body,
        mesh=mesh,
        in_specs=(tokens,) * 6 + (P("dp"),),
        out_specs=(tokens,) * 3,
        check_vma=False,
    )
```

time: 819 us -> 73.8 us (0.09); the launches traced: 806 us -> 73.6 us
  starting transfers between devices: 344 us -> 0 us
  waiting for transfers between devices: 240 us -> 0 us
  other arithmetic: 132 us -> 0 us
  Pallas kernels: 0 us -> 67.5 us
  local copies, waits for them, and re-layouts: 67.8 us -> 5.38 us
  matrix products: 12.2 us -> 0 us
  loops' own time: 10.8 us -> 0 us
    ppermute x64 -> x0, starting transfers between devices: 301 us -> none  [the longest x32 186 us: from_behind(): return lax.ppermute(array, axis, pairs)]
    ppermute x64 -> x0, waiting for transfers between devices: 194 us -> none  [the longest x32 194 us: from_behind_2(): return lax.ppermute(block, axis, route)]
    add x81 -> x0, other arithmetic: 95.9 us -> none  [the longest x16 53.1 us: travel_turn(): return (key_cur, value_cur, key_acc, value_acc, query_acc + query_term)]
    pallas_call x0 -> x1, Pallas kernels: none -> 67.5 us  [body(): pl.pallas_call(functools.partial(kernel, chips, group, rows, None), out_s...]
    while x32 -> x0, local copies, waits for them, and re-layouts: 50.1 us -> none
    all_to_all x9 -> x0, waiting for transfers between devices: 46.1 us -> none  [the longest x1 12.5 us: body(): lax.all_to_all(grad_output, 'head', split_axis=1, concat_axis=0, tiled=True)]
    all_to_all x9 -> x0, starting transfers between devices: 42.7 us -> none  [the longest x1 7.2 us: body(): lax.all_to_all(log_normalizer, 'head', split_axis=1, concat_axis=0, tiled...]
    reduce_or x16 -> x0, other arithmetic: 26.8 us -> none  [visit(): return lax.cond(jnp.any(allowed), compute_terms, empty_terms)]
  transfers between devices with their start and end apart: 73 -> 0, of which waited for: 34 -> 0; matrix products, arithmetic and copies ran while one was open for 23% -> 0% of each run, Pallas kernels for 0% -> 0%
where the time goes in v1:
time: 73.8 us; the launch traced here: 73.6 us
  Pallas kernels  67.5 us (91%)
  local copies, waits for them, and re-layouts  5.38 us (7%)
    pallas_call x1, Pallas kernels, body(): pl.pallas_call(functools.partial(kernel, chips, group, rows, None), out_s...  67.5 us
    unnamed x8, local copies, waits for them, and re-layouts  5.38 us

profile of v1, /device:TPU:1, one launch (start us, length us, event | category | flops | bytes accessed | tf_op | source)
XLA Modules:
  0.0 73.6 jit_solution(162663032943527225)
XLA Ops:
  0.6 1.4 %copy.10.lse_ref = f32[128,32]{1,0:T(8,128)} copy(f32[128,32]{0,1:T(8,128)} %param.12) | data formatting | bytes 32768 | tf_op args[5]
  2.1 67.5 %shard_map.94 = (bf16[128,4096]{1,0:T(8,128)(2,1)}, bf16[128,512]{1,0:T(8,128)(2,1)}, bf16[128,512]{1,0:T(8,128)(2,1)}) custom-call(bf16[128,4096]{1,0:T(8,128)(2,1)} %q_hbm.1, bf16[128,512]{1,0:T(8,128)(2,1)} %k_hbm.1, bf16[128,512]{1,0:T(8,128)(2,1)} %v_hbm.1, bf16[128,4096]{1,0:T(8,128)(2,1)} %o_hbm.1, bf16[128,4096]{1,0:T(8,128)(2,1)} %do_hbm.1, ...), custom_call_target="tpu_custom_call" | custom-call | flops 12079595520 | bytes 4194304 | tf_op jit(solution)/shard_map/pallas_call | solution.py:340
  69.6 0.0 copy-start.1
  69.6 2.3 %copy.14 = bf16[128,4096]{1,0:T(8,128)(2,1)} copy(bf16[128,4096]{1,0:T(8,128)(2,1)} %get-tuple-element.6) | data formatting | bytes 2097152
  72.0 0.0 copy-done.1
  72.0 0.0 copy-start
  72.0 0.7 copy.15
  72.6 0.3 copy-done
  72.9 0.7 copy.16
Async XLA Ops:
  69.6 2.3 %copy-start.1 = (bf16[128,512]{1,0:T(8,128)(2,1)S(1)}, bf16[128,512]{1,0:T(8,128)(2,1)}, u32[]{:S(2)}) copy-start(bf16[128,512]{1,0:T(8,128)(2,1)} %get-tuple-element.7) | copy-start | bytes 393220
  72.0 1.0 %copy-start = (bf16[128,512]{1,0:T(8,128)(2,1)S(1)}, bf16[128,512]{1,0:T(8,128)(2,1)}, u32[]{:S(2)}) copy-start(bf16[128,512]{1,0:T(8,128)(2,1)} %get-tuple-element.8) | copy-start | bytes 393220

commit v2 on v1

v2 whole, which is shorter than its diff:
```python
import functools

import jax
import jax.numpy as jnp
from jax import lax
from jax.experimental import pallas as pl
from jax.experimental.pallas import tpu as pltpu
from jax.sharding import PartitionSpec as P

HD = 128
LOG2E = 1.4426950408889634
SCALE = HD ** (-0.5)
HOPS = 8
MASKED = -1e30
MESH = pl.DeviceIdType.MESH
NN = (((1,), (0,)), ((), ()))
NT = (((1,), (1,)), ((), ()))
BF = jnp.bfloat16
F32 = jnp.float32


def dot(a, b, dims):
    return lax.dot_general(a, b, dims, preferred_element_type=F32)


def kernel(
    chips, group, rows, parts,
    q_hbm, k_hbm, v_hbm, o_hbm, do_hbm, lse_hbm, len_hbm,
    dq_hbm, dk_ref, dv_ref,
    lse_ref, len_ref,
    qs, dos, qt, dot_t, o_nat, do_nat, lb, db, lo_ref, pd, dqacc, dqs,
    kv, acc, pf, p8, own, h8, home, relay, sums,
    fh_send, fh_recv, ring_send, ring_recv, acc_send, acc_recv,
    home_send, home_recv, h8_send, h8_recv, own_send, own_recv,
    relay_send, relay_recv, nat_sem, q_loc, q_send, q_recv, pd_send, pd_recv, dq_loc, dq_send, dq_recv,
):
    heads = 2 * group
    block = 2 * rows
    at_ctx, at_head = lax.axis_index("ctx"), lax.axis_index("head")
    core = lax.rem(at_head, 2)
    chip = at_ctx * 2 + lax.div(at_head, 2)
    other = 1 - core
    place = lax.rem(chip, HOPS)

    def device(hop, to_core):
        to = lax.rem(chip + hop + chips, chips)
        return {"ctx": lax.div(to, 2), "head": lax.rem(to, 2) * 2 + to_core}

    def remote(src, dst, ss, rs, hop, to_core):
        return pltpu.make_async_remote_copy(
            src_ref=src, dst_ref=dst, send_sem=ss, recv_sem=rs,
            device_id=device(hop, to_core), device_id_type=MESH,
        )

    def cols(head, width=1):
        return pl.ds(pl.multiple_of(head * HD, HD), width * HD)

    def half(which):
        return pl.ds(pl.multiple_of(which * rows, rows), rows)

    barrier = pltpu.get_barrier_semaphore()
    partners = [(0, other)] + [(h, c) for h in (1, -1, 7, -7, 8, -8) for c in (0, 1)]
    for hop, c in partners:
        pl.semaphore_signal(barrier, inc=1, device_id=device(hop, c), device_id_type=MESH)
    nat = [
        pltpu.make_async_copy(o_hbm, o_nat, nat_sem.at[0]),
        pltpu.make_async_copy(do_hbm, do_nat, nat_sem.at[1]),
        pltpu.make_async_copy(lse_hbm, lse_ref, nat_sem.at[2]),
        pltpu.make_async_copy(len_hbm, len_ref, nat_sem.at[3]),
    ]
    for cp in nat:
        cp.start()

    queries = ((q_hbm, qs), (do_hbm, dos))

    @pl.loop(0, heads)
    def _(h):
        for i, (src, dst) in enumerate(queries):
            pltpu.make_async_copy(
                src.at[:, cols(heads * core + h)], dst.at[h, half(core)], q_loc.at[i]
            ).start()

    for cp in nat:
        cp.wait()
    lane = lax.broadcasted_iota(jnp.int32, (rows, 4 * group), 1)
    delta = jnp.zeros((rows, 4 * group), F32)
    for h in range(4 * group):
        at = slice(h * HD, (h + 1) * HD)
        col = jnp.sum(o_nat[:, at].astype(F32) * do_nat[:, at].astype(F32), axis=1, keepdims=True)
        delta = jnp.where(lane == h, col, delta)
    norm = lse_ref[...].T * LOG2E
    first_half = core == 0
    for i, flip in ((0, False), (1, True)):
        low = jnp.logical_xor(first_half, flip)
        pd[i, :, :heads] = jnp.where(low, norm[:, :heads], norm[:, heads:])
        pd[i, :, heads : 2 * heads] = jnp.where(low, delta[:, :heads], delta[:, heads:])
    pl.semaphore_wait(barrier, len(partners))

    kinds = [(0, 0, 1, 1), (1, 1, 1, 7), (2, 0, 0, 0), (3, 1, 8, 0), (4, 0, 8, 8), (5, 1, 0, 8)]

    def first(kind, d, which, around=False):
        _, b, slot, hop = kinds[kind]
        to_core = core if d == 0 else other
        src = (k_hbm, v_hbm)[which].at[:, cols(2 * to_core + b)]
        dst = kv.at[b, slot, which, half(core)]
        if hop == 0 and d == 0:
            return pltpu.make_async_copy(src, dst, fh_recv.at[kind, core, which])
        if kind > 3 and around:
            dst, hop = relay.at[0, b, which, half(core)], -8
        return remote(src, dst, fh_send.at[kind, d, which], fh_recv.at[kind, core, which], hop, to_core)

    def start_first(kind):
        for which in (0, 1):
            for d in (0, 1):
                if kind > 3:
                    pl.when(place != 0)(lambda: first(kind, d, which).start())
                    pl.when(place == 0)(lambda: first(kind, d, which, True).start())
                else:
                    first(kind, d, which).start()

    def wait_first(kind, which, c):
        _, b, slot, hop = kinds[kind]
        dst = kv.at[b, slot, which, pl.ds(c * rows, rows)]
        pltpu.make_async_copy(dst, dst, fh_recv.at[kind, c, which]).wait()

    def piece(ref, b, t, which, r):
        return ref.at[b, t, which, pl.ds(r * rows, rows)]

    def ring(b, t, which, r):
        return remote(
            piece(kv, b, t, which, r), piece(kv, b, t + 1, which, r),
            ring_send.at[b, t, which, r], ring_recv.at[b, t + 1, which, r], 1 - 2 * b, core,
        )

    def first_arrives(which, r):
        for b in (0, 1):
            wait_first(b, which, r)
            ring(b, 1, which, r).start()

    start_first(0)
    start_first(1)

    pd_copy = remote(pd.at[1], pd.at[2], pd_send.at[0], pd_recv.at[0], 0, other)
    pd_copy.start()

    @pl.loop(0, heads)
    def _(h):
        for i, (src, dst) in enumerate(queries):
            remote(
                src.at[:, cols(heads * other + h)], dst.at[h, half(core)],
                q_send.at[i], q_recv.at[i], 0, other,
            ).start()

    for kind in (2, 5, 3, 4):
        start_first(kind)

    row = chip * block + lax.broadcasted_iota(jnp.int32, (block, HD), 0)
    low_key = jnp.zeros((block, HD), jnp.int32)
    end = jnp.int32(0)
    for d in range(len_ref.shape[0]):
        end = end + len_ref[d]
        low_key = jnp.where(row >= end, end, low_key)
    lo_ref[...] = low_key

    dqacc[...] = jnp.zeros_like(dqacc)
    for b in (0, 1):
        acc[b, 1] = jnp.zeros(acc.shape[2:], acc.dtype)

    first_arrives(0, 0)
    first_arrives(0, 1)
    for i, (dst, turned) in enumerate(((qs, qt), (dos, dot_t))):
        mine = dst.at[:, half(core)]
        theirs = dst.at[:, half(other)]
        pltpu.make_async_copy(mine, mine, q_loc.at[i]).wait()
        pltpu.make_async_copy(theirs, theirs, q_recv.at[i]).wait()
        for h in range(heads):
            turned[:, h * block : (h + 1) * block] = dst[h].T
        first_arrives(1, i)
    pd_copy.wait_recv()
    for i, at in ((0, core), (2, other)):
        for h in range(heads):
            lb[h, half(at)] = jnp.broadcast_to(pd[i, :, h : h + 1], (rows, HD))
            db[h, half(at)] = jnp.broadcast_to(pd[i, :, heads + h : heads + h + 1], (rows, HD))

    def pass_on(b, t, which, r):
        return remote(
            acc.at[b, t, which, r], acc.at[b, t + 1, which, r],
            acc_send.at[b, t, which, r], acc_recv.at[b, t + 1, which, r], 1 - 2 * b, core,
        )

    def go_home(b, which, r):
        return remote(
            acc.at[b, HOPS - 1, which, r], home.at[b, core, which],
            home_send.at[b, r, which], home_recv.at[b, core, which], -7 if b == 0 else -1, r,
        )

    def far_home(b, which, r):
        return remote(
            p8.at[b, which, r], h8.at[b, core, which],
            h8_send.at[b, r, which], h8_recv.at[b, core, which], -8, r,
        )

    def passing(stage, b, hop):
        src = relay.at[stage, b]
        dst = relay.at[1, b] if stage == 0 else kv.at[b, HOPS * (1 - b)]
        return remote(src, dst, relay_send.at[stage, b], relay_recv.at[stage, b], hop, core)

    def keys_stage(stage, b):
        @pl.when(place == 0)
        def _():
            if stage == 0:
                for which in (0, 1):
                    for c in (0, 1):
                        wait_first(4 + b, which, c)
            else:
                passing(0, b, -8).wait_recv()
            passing(stage, b, -8).start()

    def sums_out(stage, b):
        src = p8.at[b] if stage == 0 else sums.at[0, b]
        return remote(
            src, sums.at[stage, b], relay_send.at[stage, b], relay_recv.at[stage, b], 8, core
        )

    def sums_home(b, which, r):
        return remote(
            sums.at[1, b, which, r], h8.at[b, core, which],
            h8_send.at[b, r, which], h8_recv.at[b, core, which], 8, r,
        )

    def sums_stage(stage, b):
        @pl.when(place == HOPS - 1)
        def _():
            sums_out(stage - 1, b).wait_recv()
            if stage == 1:
                sums_out(1, b).start()
            else:
                for which in (0, 1):
                    for r in (0, 1):
                        sums_home(b, which, r).start()

    def own_home(b, which):
        return remote(
            pf.at[1, b, which, other], own.at[b, core, which],
            own_send.at[b, which], own_recv.at[b, which], 0, other,
        )

    step = group // 2

    def wide(x):
        return jnp.concatenate([x] * (block // HD), axis=-1) if block >= HD else x[..., :block]

    def chunk(b, slot, distance, to):
        keys = kv[b, slot, 0]
        values = kv[b, slot, 1]
        key_at = (chip - distance) * block + lax.broadcasted_iota(jnp.int32, (block, block), 1)
        row_at = chip * block + lax.broadcasted_iota(jnp.int32, (block, block), 0)
        bias = jnp.where((key_at >= wide(lo_ref[...])) & (key_at <= row_at), 0.0, MASKED)
        dk_t = jnp.zeros((HD, block), F32)
        dv_t = jnp.zeros((HD, block), F32)
        for h in range(b * group, (b + 1) * group, step):
            some = slice(h, h + step)
            flat = slice(h * block, (h + step) * block)
            q = qs[some].reshape(step * block, HD)
            g = dos[some].reshape(step * block, HD)
            s = dot(q, keys, NT).reshape(step, block, block)
            dp = dot(g, values, NT).reshape(step, block, block)
            p = jnp.exp2(s * (SCALE * LOG2E) - wide(lb[some]) + bias[None])
            ds = (p * (dp - wide(db[some]))).astype(BF).reshape(step * block, block)
            ph = p.astype(BF).reshape(step * block, block)
            dv_t = dv_t + dot(dot_t[:, flat], ph, NN)
            dk_t = dk_t + dot(qt[:, flat], ds, NN)
            dqacc[some] += dot(ds, keys, NN).reshape(step, block, HD)
        for which, part in enumerate((dk_t, dv_t)):
            for r in (0, 1):
                pf[to, b, which, r] = part[:, r * rows : (r + 1) * rows]

    def own_block(b):
        for which in (0, 1):
            for c in (0, 1):
                wait_first(2 + b, which, c)
        chunk(b, HOPS * b, 0, 1)
        for which in (0, 1):
            own_home(b, which).start()
            own[b, core, which] = pf[1, b, which, core]

    def far_block(b):
        @pl.when(place != 0)
        def _():
            for which in (0, 1):
                for c in (0, 1):
                    wait_first(4 + b, which, c)

        @pl.when(place == 0)
        def _():
            passing(1, b, -8).wait_recv()

        chunk(b, HOPS * (1 - b), HOPS, 2)
        p8[b] = pf[2, b].astype(BF)

        @pl.when(place != HOPS - 1)
        def _():
            for which in (0, 1):
                for r in (0, 1):
                    far_home(b, which, r).start()

        @pl.when(place == HOPS - 1)
        def _():
            sums_out(0, b).start()

    own_block(0)
    keys_stage(0, 0)

    @pl.loop(1, HOPS)
    def _(t):
        def arrives(which, r):
            @pl.when(t < HOPS - 1)
            def _():
                for b in (0, 1):
                    ring(b, t, which, r).wait_recv()

                    @pl.when(t < HOPS - 2)
                    def _():
                        ring(b, t + 1, which, r).start()

        def add(which):
            for r in (0, 1):
                for b in (0, 1):
                    @pl.when(t > 1)
                    def _():
                        pass_on(b, t - 1, which, r).wait_recv()

                    acc[b, t, which, r] = (acc[b, t, which, r].astype(F32) + pf[0, b, which, r]).astype(BF)

                    @pl.when(t < HOPS - 1)
                    def _():
                        pass_on(b, t, which, r).start()

                    @pl.when(t == HOPS - 1)
                    def _():
                        go_home(b, which, r).start()

        chunk(0, t, t, 0)
        arrives(0, 0)
        arrives(0, 1)
        chunk(1, t, HOPS - t, 0)
        arrives(1, 0)
        add(0)
        add(1)
        pl.when(t == 2)(lambda: own_block(1))
        pl.when(t == 3)(lambda: far_block(0))
        pl.when(t == 4)(lambda: far_block(1))
        arrives(1, 1)

        @pl.when(t == 1)
        def _():
            keys_stage(0, 1)
            keys_stage(1, 0)

        pl.when(t == 2)(lambda: keys_stage(1, 1))
        pl.when(t == 4)(lambda: sums_stage(1, 0))

        @pl.when(t == 5)
        def _():
            sums_stage(2, 0)
            sums_stage(1, 1)

        pl.when(t == 6)(lambda: sums_stage(2, 1))

    dqs[...] = (dqacc[...] * SCALE).astype(BF)

    @pl.loop(0, heads)
    def _(h):
        pltpu.make_async_copy(
            dqs.at[h, half(core)], dq_hbm.at[:, cols(heads * core + h)], dq_loc.at[0]
        ).start()
        remote(
            dqs.at[h, half(other)], dq_hbm.at[:, cols(heads * core + h)],
            dq_send.at[0], dq_recv.at[0], 0, other,
        ).start()

    for b in (0, 1):
        for which in (0, 1):
            got = own.at[b, other, which]
            pltpu.make_async_copy(got, got, own_recv.at[b, which]).wait()
            for c in (0, 1):
                for buf, sems in ((h8, h8_recv), (home, home_recv)):
                    got = buf.at[b, c, which]
                    pltpu.make_async_copy(got, got, sems.at[b, c, which]).wait()
    for c in (0, 1):
        for b in (0, 1):
            at = slice((2 * c + b) * HD, (2 * c + b + 1) * HD)
            total = [
                own[b, c, which] + h8[b, c, which].astype(F32) + home[b, c, which].astype(F32)
                for which in (0, 1)
            ]
            dk_ref[:, at] = (total[0] * SCALE).T.astype(BF)
            dv_ref[:, at] = total[1].T.astype(BF)

    for i, dst in enumerate((qs, dos)):
        out = dst.at[:, half(core)]
        pltpu.make_async_copy(out, out, q_send.at[i]).wait()
    pd_copy.wait_send()
    for kind in range(6):
        for which in (0, 1):
            for d in (0, 1):
                if not (kinds[kind][3] == 0 and d == 0):
                    first(kind, d, which).wait_send()
    @pl.when((place == 0) | (place == HOPS - 1))
    def _():
        for b in (0, 1):
            for stage in (0, 1):
                passing(stage, b, 8).wait_send()

    for b in (0, 1):
        for which in (0, 1):
            for r in (0, 1):
                far_home(b, which, r).wait_send()
                go_home(b, which, r).wait_send()
                for t in range(1, HOPS - 1):
                    ring(b, t, which, r).wait_send()
                    pass_on(b, t, which, r).wait_send()
            own_home(b, which).wait_send()
    out = dq_hbm.at[:, cols(heads * core, heads)]
    pltpu.make_async_copy(out, out, dq_loc.at[0]).wait()
    pltpu.make_async_copy(out, out, dq_send.at[0]).wait()
    got = dq_hbm.at[:, cols(heads * other, heads)]
    pltpu.make_async_copy(got, got, dq_recv.at[0]).wait()


def finish(dq, dk, dv, dq_out, dk_out, dv_out, sems):
    copies = [
        pltpu.make_async_copy(a, b, sems.at[i])
        for i, (a, b) in enumerate(((dq, dq_out), (dk, dk_out), (dv, dv_out)))
    ]
    for cp in copies:
        cp.start()
    for cp in copies:
        cp.wait()


def body(query_rows, key_rows, value_rows, fwd_output, grad_output, log_normalizer, doc_lengths):
    rows = query_rows.shape[0]
    group = query_rows.shape[1] // key_rows.shape[1]
    chips = lax.axis_size("ctx") * 2
    heads = 2 * group
    block = 2 * rows
    any_space = pl.BlockSpec(memory_space=pl.ANY)
    vmem = pl.BlockSpec(memory_space=pltpu.VMEM)
    dma = pltpu.SemaphoreType.DMA
    slots = HOPS + 1
    flops = 2 * slots * group * block * block * HD * 2 * 5
    grads = pl.pallas_call(
        functools.partial(kernel, chips, group, rows, None),
        out_shape=[
            pltpu.VMEM(query_rows.shape, BF),
            pltpu.VMEM(key_rows.shape, BF),
            pltpu.VMEM(value_rows.shape, BF),
        ],
        in_specs=[any_space] * 7,
        out_specs=[vmem, vmem, vmem],
        scratch_shapes=[
            pltpu.VMEM((2 * heads, rows), F32),
            pltpu.SMEM(doc_lengths.shape, jnp.int32),
            pltpu.VMEM((heads, block, HD), BF),
            pltpu.VMEM((heads, block, HD), BF),
            pltpu.VMEM((HD, heads * block), BF),
            pltpu.VMEM((HD, heads * block), BF),
            pltpu.VMEM((rows, 2 * heads * HD), BF),
            pltpu.VMEM((rows, 2 * heads * HD), BF),
            pltpu.VMEM((heads, block, HD), F32),
            pltpu.VMEM((heads, block, HD), F32),
            pltpu.VMEM((block, HD), jnp.int32),
            pltpu.VMEM((3, rows, HD), F32),
            pltpu.VMEM((heads, block, HD), F32),
            pltpu.VMEM((heads, block, HD), BF),
            pltpu.VMEM((2, slots, 2, block, HD), BF),
            pltpu.VMEM((2, HOPS, 2, 2, HD, rows), BF),
            pltpu.VMEM((3, 2, 2, 2, HD, rows), F32),
            pltpu.VMEM((2, 2, 2, HD, rows), BF),
            pltpu.VMEM((2, 2, 2, HD, rows), F32),
            pltpu.VMEM((2, 2, 2, HD, rows), BF),
            pltpu.VMEM((2, 2, 2, HD, rows), BF),
            pltpu.VMEM((2, 2, 2, block, HD), BF),
            pltpu.VMEM((2, 2, 2, 2, HD, rows), BF),
            dma((6, 2, 2)), dma((6, 2, 2)),
            dma((2, slots, 2, 2)), dma((2, slots, 2, 2)),
            dma((2, slots, 2, 2)), dma((2, slots, 2, 2)),
            dma((2, 2, 2)), dma((2, 2, 2)),
            dma((2, 2, 2)), dma((2, 2, 2)),
            dma((2, 2)), dma((2, 2)),
            dma((2, 2)), dma((2, 2)),
            dma((4,)), dma((2,)), dma((2,)), dma((2,)),
            dma((1,)), dma((1,)), dma((1,)), dma((1,)), dma((1,)),
        ],
        compiler_params=pltpu.CompilerParams(
            collective_id=0, has_side_effects=True, vmem_limit_bytes=48 * 2**20
        ),
        cost_estimate=pl.CostEstimate(
            flops=flops, bytes_accessed=8 * rows * 2 * heads * HD, transcendentals=flops // (10 * HD)
        ),
    )(
        *(
            pltpu.with_memory_space_constraint(x, pltpu.HBM)
            for x in (query_rows, key_rows, value_rows, fwd_output, grad_output, log_normalizer.T, doc_lengths)
        )
    )
    return pl.pallas_call(
        finish,
        out_shape=[jax.ShapeDtypeStruct(x.shape, x.dtype) for x in (query_rows, key_rows, value_rows)],
        in_specs=[vmem] * 3,
        out_specs=[any_space] * 3,
        scratch_shapes=[dma((3,))],
    )(*(pltpu.with_memory_space_constraint(x, pltpu.VMEM) for x in grads))


def solution(mesh):
    tokens = P(("dp", "ctx", "head"), None)
    return jax.shard_map(
        body,
        mesh=mesh,
        in_specs=(tokens,) * 6 + (P("dp"),),
        out_specs=(tokens,) * 3,
        check_vma=False,
    )
```

time: 73.8 us -> 66.4 us (0.90)
  local copies, waits for them, and re-layouts: 5.38 us -> 0 us
  Pallas kernels: 67.5 us -> 65.7 us
    unnamed x8 -> x0, local copies, waits for them, and re-layouts: 5.38 us -> none
    pallas_call x1, Pallas kernels: 67.5 us -> 64.6 us  [body(): pl.pallas_call(functools.partial(kernel, chips, group, rows, None), out_s...]
    pallas_call x0 -> x1, Pallas kernels: none -> 1.07 us  [body(): pl.pallas_call(finish, out_shape=[jax.ShapeDtypeStruct(x.shape, x.dtype)...]
where the time goes in v2:
time: 66.4 us; the launch traced here: 66.3 us
  Pallas kernels  65.7 us (99%)
    pallas_call x1, Pallas kernels, body(): pl.pallas_call(functools.partial(kernel, chips, group, rows, None), out_s...  64.6 us

profile of v2, /device:TPU:1, one launch (start us, length us, event | category | flops | bytes accessed | tf_op | source)
XLA Modules:
  0.0 66.3 jit_solution(2174286634192780418)
XLA Ops:
  0.6 64.6 %shard_map.94 = (bf16[128,4096]{1,0:T(8,128)(2,1)S(1)}, bf16[128,512]{1,0:T(8,128)(2,1)S(1)}, bf16[128,512]{1,0:T(8,128)(2,1)S(1)}) custom-call(bf16[128,4096]{1,0:T(8,128)(2,1)} %q_hbm.1, bf16[128,512]{1,0:T(8,128)(2,1)} %k_hbm.1, bf16[128,512]{1,0:T(8,128)(2,1)} %v_hbm.1, bf16[128,4096]{1,0:T(8,128)(2,1)} %o_hbm.1, bf16[128,4096]{1,0:T(8,128)(2,1)} %do_hbm.1, ...), custom_call_target="tpu_custom_call" | custom-call | flops 12079595520 | bytes 4194304 | tf_op jit(solution)/shard_map/pallas_call | solution.py:453
  65.3 1.1 %shard_map.95 = (bf16[128,4096]{1,0:T(8,128)(2,1)}, bf16[128,512]{1,0:T(8,128)(2,1)}, bf16[128,512]{1,0:T(8,128)(2,1)}) custom-call(bf16[128,4096]{1,0:T(8,128)(2,1)S(1)} %get-tuple-element.6.dq, bf16[128,512]{1,0:T(8,128)(2,1)S(1)} %get-tuple-element.7.dk, bf16[128,512]{1,0:T(8,128)(2,1)S(1)} %get-tuple-element.8.dv), custom_call_target="tpu_custom_call" | custom-call | tf_op jit(solution)/shard_map/pallas_call | solution.py:508

commit v3 on v2

--- a/solution.py
+++ b/solution.py
@@ -94,6 +94,17 @@
         low = jnp.logical_xor(first_half, flip)
         pd[i, :, :heads] = jnp.where(low, norm[:, :heads], norm[:, heads:])
         pd[i, :, heads : 2 * heads] = jnp.where(low, delta[:, :heads], delta[:, heads:])
+    row = chip * block + lax.broadcasted_iota(jnp.int32, (block, HD), 0)
+    low_key = jnp.zeros((block, HD), jnp.int32)
+    end = jnp.int32(0)
+    for d in range(len_ref.shape[0]):
+        end = end + len_ref[d]
+        low_key = jnp.where(row >= end, end, low_key)
+    lo_ref[...] = low_key
+
+    dqacc[...] = jnp.zeros_like(dqacc)
+    for b in (0, 1):
+        acc[b, 1] = jnp.zeros(acc.shape[2:], acc.dtype)
     pl.semaphore_wait(barrier, len(partners))
 
     kinds = [(0, 0, 1, 1), (1, 1, 1, 7), (2, 0, 0, 0), (3, 1, 8, 0), (4, 0, 8, 8), (5, 1, 0, 8)]
@@ -151,20 +162,8 @@
                 q_send.at[i], q_recv.at[i], 0, other,
             ).start()
 
-    for kind in (2, 5, 3, 4):
+    for kind in (2, 4, 3, 5):
         start_first(kind)
-
-    row = chip * block + lax.broadcasted_iota(jnp.int32, (block, HD), 0)
-    low_key = jnp.zeros((block, HD), jnp.int32)
-    end = jnp.int32(0)
-    for d in range(len_ref.shape[0]):
-        end = end + len_ref[d]
-        low_key = jnp.where(row >= end, end, low_key)
-    lo_ref[...] = low_key
-
-    dqacc[...] = jnp.zeros_like(dqacc)
-    for b in (0, 1):
-        acc[b, 1] = jnp.zeros(acc.shape[2:], acc.dtype)
 
     first_arrives(0, 0)
     first_arrives(0, 1)
@@ -362,10 +361,10 @@
 
         @pl.when(t == 5)
         def _():
+            sums_stage(1, 1)
             sums_stage(2, 0)
-            sums_stage(1, 1)
-
-        pl.when(t == 6)(lambda: sums_stage(2, 1))
+
+        pl.when(t == HOPS - 1)(lambda: sums_stage(2, 1))
 
     dqs[...] = (dqacc[...] * SCALE).astype(BF)
 

time: 66.4 us -> 63.4 us (0.955)
  Pallas kernels: 65.7 us -> 62.6 us
    pallas_call x1, Pallas kernels: 64.6 us -> 61.6 us  [body(): pl.pallas_call(functools.partial(kernel, chips, group, rows, None), out_s...]
where the time goes in v3:
time: 63.4 us; the launch traced here: 63.3 us
  Pallas kernels  62.6 us (99%)
  between operations  0.64 us (1%)
    pallas_call x1, Pallas kernels, body(): pl.pallas_call(functools.partial(kernel, chips, group, rows, None), out_s...  61.6 us

profile of v3, /device:TPU:1, one launch (start us, length us, event | category | flops | bytes accessed | tf_op | source)
XLA Modules:
  0.0 63.3 jit_solution(2984490780431088130)
XLA Ops:
  0.6 61.6 %shard_map.94 = (bf16[128,4096]{1,0:T(8,128)(2,1)S(1)}, bf16[128,512]{1,0:T(8,128)(2,1)S(1)}, bf16[128,512]{1,0:T(8,128)(2,1)S(1)}) custom-call(bf16[128,4096]{1,0:T(8,128)(2,1)} %q_hbm.1, bf16[128,512]{1,0:T(8,128)(2,1)} %k_hbm.1, bf16[128,512]{1,0:T(8,128)(2,1)} %v_hbm.1, bf16[128,4096]{1,0:T(8,128)(2,1)} %o_hbm.1, bf16[128,4096]{1,0:T(8,128)(2,1)} %do_hbm.1, ...), custom_call_target="tpu_custom_call" | custom-call | flops 12079595520 | bytes 4194304 | tf_op jit(solution)/shard_map/pallas_call | solution.py:452
  62.2 1.1 %shard_map.95 = (bf16[128,4096]{1,0:T(8,128)(2,1)}, bf16[128,512]{1,0:T(8,128)(2,1)}, bf16[128,512]{1,0:T(8,128)(2,1)}) custom-call(bf16[128,4096]{1,0:T(8,128)(2,1)S(1)} %get-tuple-element.6.dq, bf16[128,512]{1,0:T(8,128)(2,1)S(1)} %get-tuple-element.7.dk, bf16[128,512]{1,0:T(8,128)(2,1)S(1)} %get-tuple-element.8.dv), custom_call_target="tpu_custom_call" | custom-call | tf_op jit(solution)/shard_map/pallas_call | solution.py:507

commit v4 on v3

--- a/solution.py
+++ b/solution.py
@@ -244,7 +244,7 @@
             own_send.at[b, which], own_recv.at[b, which], 0, other,
         )
 
-    step = group // 2
+    step = group
 
     def wide(x):
         return jnp.concatenate([x] * (block // HD), axis=-1) if block >= HD else x[..., :block]
@@ -345,10 +345,10 @@
         chunk(1, t, HOPS - t, 0)
         arrives(1, 0)
         add(0)
-        add(1)
         pl.when(t == 2)(lambda: own_block(1))
         pl.when(t == 3)(lambda: far_block(0))
         pl.when(t == 4)(lambda: far_block(1))
+        add(1)
         arrives(1, 1)
 
         @pl.when(t == 1)
@@ -378,24 +378,6 @@
             dq_send.at[0], dq_recv.at[0], 0, other,
         ).start()
 
-    for b in (0, 1):
-        for which in (0, 1):
-            got = own.at[b, other, which]
-            pltpu.make_async_copy(got, got, own_recv.at[b, which]).wait()
-            for c in (0, 1):
-                for buf, sems in ((h8, h8_recv), (home, home_recv)):
-                    got = buf.at[b, c, which]
-                    pltpu.make_async_copy(got, got, sems.at[b, c, which]).wait()
-    for c in (0, 1):
-        for b in (0, 1):
-            at = slice((2 * c + b) * HD, (2 * c + b + 1) * HD)
-            total = [
-                own[b, c, which] + h8[b, c, which].astype(F32) + home[b, c, which].astype(F32)
-                for which in (0, 1)
-            ]
-            dk_ref[:, at] = (total[0] * SCALE).T.astype(BF)
-            dv_ref[:, at] = total[1].T.astype(BF)
-
     for i, dst in enumerate((qs, dos)):
         out = dst.at[:, half(core)]
         pltpu.make_async_copy(out, out, q_send.at[i]).wait()
@@ -405,6 +387,7 @@
             for d in (0, 1):
                 if not (kinds[kind][3] == 0 and d == 0):
                     first(kind, d, which).wait_send()
+
     @pl.when((place == 0) | (place == HOPS - 1))
     def _():
         for b in (0, 1):
@@ -414,12 +397,33 @@
     for b in (0, 1):
         for which in (0, 1):
             for r in (0, 1):
-                far_home(b, which, r).wait_send()
-                go_home(b, which, r).wait_send()
                 for t in range(1, HOPS - 1):
                     ring(b, t, which, r).wait_send()
                     pass_on(b, t, which, r).wait_send()
             own_home(b, which).wait_send()
+
+    for b in (0, 1):
+        for which in (0, 1):
+            got = own.at[b, other, which]
+            pltpu.make_async_copy(got, got, own_recv.at[b, which]).wait()
+    for which in (0, 1):
+        for b in (0, 1):
+            for c in (0, 1):
+                for buf, sems in ((h8, h8_recv), (home, home_recv)):
+                    got = buf.at[b, c, which]
+                    pltpu.make_async_copy(got, got, sems.at[b, c, which]).wait()
+                at = slice((2 * c + b) * HD, (2 * c + b + 1) * HD)
+                total = own[b, c, which] + h8[b, c, which].astype(F32) + home[b, c, which].astype(F32)
+                if which == 0:
+                    dk_ref[:, at] = (total * SCALE).T.astype(BF)
+                else:
+                    dv_ref[:, at] = total.T.astype(BF)
+
+    for b in (0, 1):
+        for which in (0, 1):
+            for r in (0, 1):
+                far_home(b, which, r).wait_send()
+                go_home(b, which, r).wait_send()
     out = dq_hbm.at[:, cols(heads * core, heads)]
     pltpu.make_async_copy(out, out, dq_loc.at[0]).wait()
     pltpu.make_async_copy(out, out, dq_send.at[0]).wait()

time: 63.4 us -> 63.3 us (level)
  no operation moved by 1% of the time
where the time goes in v4:
time: 63.3 us; the launch traced here: 63.2 us
  Pallas kernels  62.5 us (99%)
  between operations  0.64 us (1%)
    pallas_call x1, Pallas kernels, body(): pl.pallas_call(functools.partial(kernel, chips, group, rows, None), out_s...  61.5 us

profile of v4, /device:TPU:1, one launch (start us, length us, event | category | flops | bytes accessed | tf_op | source)
XLA Modules:
  0.0 63.2 jit_solution(13293955090599822)
XLA Ops:
  0.6 61.5 %shard_map.94 = (bf16[128,4096]{1,0:T(8,128)(2,1)S(1)}, bf16[128,512]{1,0:T(8,128)(2,1)S(1)}, bf16[128,512]{1,0:T(8,128)(2,1)S(1)}) custom-call(bf16[128,4096]{1,0:T(8,128)(2,1)} %q_hbm.1, bf16[128,512]{1,0:T(8,128)(2,1)} %k_hbm.1, bf16[128,512]{1,0:T(8,128)(2,1)} %v_hbm.1, bf16[128,4096]{1,0:T(8,128)(2,1)} %o_hbm.1, bf16[128,4096]{1,0:T(8,128)(2,1)} %do_hbm.1, ...), custom_call_target="tpu_custom_call" | custom-call | flops 12079595520 | bytes 4194304 | tf_op jit(solution)/shard_map/pallas_call | solution.py:456
  62.1 1.1 %shard_map.95 = (bf16[128,4096]{1,0:T(8,128)(2,1)}, bf16[128,512]{1,0:T(8,128)(2,1)}, bf16[128,512]{1,0:T(8,128)(2,1)}) custom-call(bf16[128,4096]{1,0:T(8,128)(2,1)S(1)} %get-tuple-element.6.dq, bf16[128,512]{1,0:T(8,128)(2,1)S(1)} %get-tuple-element.7.dk, bf16[128,512]{1,0:T(8,128)(2,1)S(1)} %get-tuple-element.8.dv), custom_call_target="tpu_custom_call" | custom-call | tf_op jit(solution)/shard_map/pallas_call | solution.py:511
